TPU v7x, 512 devices: a whole 4x4x16 slice. The times are simulated.
512 devices in a mesh: line: 4 (over y), tile: 8 (over x, core), row: 16 (over z).
Axes of the slice: x: 4, y: 4, z: 16, core: 2. Of those that a mesh axis runs over, the one named last changes fastest.
Arguments:
- cells: int32 [65536, 128], P(('line', 'tile', 'row')), may hold values from 0 to 8191
- heights: float32 [65536, 128], P(('line', 'tile', 'row')), may hold values from -24 to 24
- weights: float32 [65536, 128], P(('line', 'tile', 'row')), may hold values from 0.25 to 4
- dest: int32 [65536], P(('line', 'tile', 'row')), may hold values from 0 to 127, as said below
- counts: int32 [4, 8, 16], P('line', 'tile', 'row'), may hold values from 64 to 128, as said below
- prefire_elevation: float32 [1024, 1024], P('row', 'tile'), may hold values from -6 to 6
Outputs:
- elevation_change: float32 [1024, 1024], P('row', 'tile')
Inputs may be any that keep to these rules, and one draw needn't show every extreme that they name: `dest`: among the 128 blocks of one device, live or not, at most 2 name any one tile; in every draw one tile is named by exactly 2 blocks of every device. `counts`: the live blocks of a device are its first ones; some device has all its blocks live.
All inputs are finite; a program needn't handle non-finite values.
Results may differ from a plain program's by a relative error of at most 0.0018.
Values sent between devices are 32-bit elements; how exact they have to be, the bound alone decides.
No kernel may reach another device: no remote copies, remote signals or barrier semaphores. Data moves between devices by JAX's collectives and lax.ppermute only.
A program may use at most 64 MiB of HBM per device.

v0:
```python
import jax
import jax.numpy as jnp
from jax import lax
from jax.sharding import PartitionSpec as P


def padded(x, sides, width):
    for axis, dim in sides:
        devices, length = (lax.axis_size(axis), x.shape[dim])
        up = [(i, (i + 1) % devices) for i in range(devices - 1)]
        down = [(j, i) for i, j in up]
        last = lax.slice_in_dim(x, length - width, length, axis=dim)
        initial = lax.slice_in_dim(x, 0, width, axis=dim)
        before = lax.ppermute(last, axis, up)
        after = lax.ppermute(initial, axis, down)
        x = jnp.concatenate([before, x, after], axis=dim)
    return x


def kernel_weight(di, dj):
    if di == 0 and dj == 0:
        return 2.0
    return 1.0 / (di * di + dj * dj)


def bin_points(point_cells, value_wz, value_w, tile_row_count, tile_column_count):
    total = point_cells.shape[0]
    group = min(total, 4096)
    steps_count = total // group
    cells_blocks = point_cells.reshape(steps_count, group)
    wz_blocks = value_wz.reshape(steps_count, group)
    w_blocks = value_w.reshape(steps_count, group)
    row_ids = lax.iota(jnp.int32, tile_row_count)
    col_ids = lax.iota(jnp.int32, tile_column_count)

    def add_block(acc, item):
        cell_ids, block_wz, block_w = item
        row_hot = ((cell_ids // tile_column_count)[:, None] == row_ids[None, :]).astype(
            jnp.bfloat16
        )
        col_hot = ((cell_ids % tile_column_count)[:, None] == col_ids[None, :]).astype(jnp.bfloat16)
        right = jnp.concatenate([col_hot * block_wz[:, None], col_hot * block_w[:, None]], axis=1)
        part_sum = lax.dot_general(
            row_hot, right, (((0,), (0,)), ((), ())), preferred_element_type=jnp.float32
        )
        return (acc + part_sum, None)

    start = jnp.zeros((tile_row_count, 2 * tile_column_count), jnp.float32)
    sums, _ = lax.scan(add_block, start, (cells_blocks, wz_blocks, w_blocks))
    return jnp.stack([sums[:, :tile_column_count], sums[:, tile_column_count:]], axis=0)


def per_device(cells, heights, weights, dest, counts, prefire_elevation):
    blocks_here = dest.shape[0]
    block_len = cells.shape[1]
    tile_row_count = prefire_elevation.shape[0]
    tile_column_count = prefire_elevation.shape[1]
    tiles_all = lax.axis_size(("tile", "row"))
    capacity = 2 * blocks_here // tiles_all
    live = lax.iota(jnp.int32, blocks_here) < counts.reshape(-1)[0]
    onehot = ((dest[:, None] == lax.iota(jnp.int32, tiles_all)[None, :]) & live[:, None]).astype(
        jnp.int32
    )
    earlier = jnp.cumsum(onehot, axis=0) - onehot
    rank_in = jnp.sum(earlier * onehot, axis=1)
    slot_index = jnp.where(live, dest * capacity + rank_in, tiles_all * capacity)
    payload = jnp.stack([heights, weights], axis=1)
    send_vals = (
        jnp.zeros((tiles_all * capacity + 1, 2, block_len), jnp.float32)
        .at[slot_index]
        .set(payload)[:-1]
    )
    send_cells = (
        jnp.zeros((tiles_all * capacity + 1, block_len), jnp.int32).at[slot_index].set(cells)[:-1]
    )
    recv_vals, recv_cells = (
        lax.all_to_all(
            send_vals.reshape(tiles_all, capacity, 2, block_len),
            ("tile", "row"),
            split_axis=0,
            concat_axis=0,
            tiled=True,
        ),
        lax.all_to_all(
            send_cells.reshape(tiles_all, capacity, block_len),
            ("tile", "row"),
            split_axis=0,
            concat_axis=0,
            tiled=True,
        ),
    )
    recv_vals = recv_vals.reshape(-1, 2, block_len)
    point_heights = recv_vals[:, 0, :].reshape(-1)
    point_weights = recv_vals[:, 1, :].reshape(-1)
    point_cells = recv_cells.reshape(-1)
    value_wz = (point_weights * point_heights).astype(jnp.bfloat16)
    value_w = point_weights.astype(jnp.bfloat16)
    partial_value = bin_points(point_cells, value_wz, value_w, tile_row_count, tile_column_count)
    summed = lax.psum(partial_value, "line")
    widened = padded(summed, (("tile", 2), ("row", 1)), 2)
    weighted_height_sum = jnp.zeros((tile_row_count, tile_column_count), jnp.float32)
    weight_total = jnp.zeros((tile_row_count, tile_column_count), jnp.float32)
    for di in range(-2, 3):
        for dj in range(-2, 3):
            factor = kernel_weight(di, dj)
            weighted_height_sum = (
                weighted_height_sum
                + factor
                * widened[0, 2 + di : 2 + di + tile_row_count, 2 + dj : 2 + dj + tile_column_count]
            )
            weight_total = (
                weight_total
                + factor
                * widened[1, 2 + di : 2 + di + tile_row_count, 2 + dj : 2 + dj + tile_column_count]
            )
    filled_cells = (weighted_height_sum + 16.0 * prefire_elevation) / (weight_total + 16.0)
    return filled_cells - prefire_elevation


def solution(mesh):
    placed = (
        P(("line", "tile", "row"), None),
        P(("line", "tile", "row"), None),
        P(("line", "tile", "row"), None),
        P(("line", "tile", "row")),
        P("line", "tile", "row"),
        P("row", "tile"),
    )
    return jax.shard_map(
        per_device, mesh=mesh, in_specs=placed, out_specs=P("row", "tile"), check_vma=False
    )
```

profile of v0, /device:TPU:1, one launch (start us, length us, event | category | flops | bytes accessed | tf_op | source)
XLA Modules:
  0.0 181.7 jit_solution(3121588694363412474)
XLA Ops:
  9.6 1.2 scatter_custom_fusion
  11.5 20.4 %all-to-all-start = ((s32[128,2,128]{2,1,0:T(2,128)}), s32[128,2,128]{2,1,0:T(2,128)S(1)}, u32[]{:S(2)}, u32[]{:S(2)}) async-start(s32[128,2,128]{2,1,0:T(2,128)} %bitcast.1), calls=%async_computation | async-start | bytes 262144 | tf_op jit(solution)/shard_map/all_to_all | solution.py:84
  33.0 4.4 %scatter_fusion = f32[257,2,128]{2,1,0:T(2,128)S(1)} fusion(f32[257,2,128]{2,1,0:T(2,128)S(1)} %broadcast_in_dim.30, s32[128]{0:T(128)S(1)} %compare_select_fusion, f32[128,2,128]{2,1,0:T(2,128)S(1)} %copy.7), kind=kCustom, calls=%fused_computation.1 | custom fusion | bytes 393728 | tf_op jit(solution)/shard_map/scatter | solution.py:71
  38.1 12.0 %all-to-all-done = s32[128,2,128]{2,1,0:T(2,128)S(1)} async-done(((s32[128,2,128]{2,1,0:T(2,128)}), s32[128,2,128]{2,1,0:T(2,128)S(1)}, u32[]{:S(2)}, u32[]{:S(2)}) %all-to-all-start) | async-done | bytes 131104 | tf_op jit(solution)/shard_map/all_to_all | solution.py:84
  50.1 5.3 %all-to-all-start.1 = ((f32[128,2,2,128]{3,2,1,0:T(2,128)}), f32[128,2,2,128]{3,2,1,0:T(2,128)S(1)}, u32[]{:S(2)}, u32[]{:S(2)}) async-start(f32[128,2,2,128]{3,2,1,0:T(2,128)} %bitcast.4), calls=%async_computation.1 | async-start | bytes 524288 | tf_op jit(solution)/shard_map/all_to_all | solution.py:77
  55.6 22.9 %all-to-all-done.1 = f32[128,2,2,128]{3,2,1,0:T(2,128)S(1)} async-done(((f32[128,2,2,128]{3,2,1,0:T(2,128)}), f32[128,2,2,128]{3,2,1,0:T(2,128)S(1)}, u32[]{:S(2)}, u32[]{:S(2)}) %all-to-all-start.1) | async-done | bytes 262176 | tf_op jit(solution)/shard_map/all_to_all | solution.py:77
  78.8 27.6 %while.13 = (s32[]{:T(128)}, f32[64,256]{1,0:T(8,128)S(1)}, s32[8,4096]{1,0:T(8,128)S(1)}, bf16[8,4096]{1,0:T(8,128)(2,1)S(1)}, bf16[8,4096]{1,0:T(8,128)(2,1)S(1)}, /*index=5*/s32[]{:T(128)}, s32[]{:T(128)}) while((s32[]{:T(128)}, f32[64,256]{1,0:T(8,128)S(1)}, s32[8,4096]{1,0:T(8,128)S(1)}, bf16[8,4096]{1,0:T(8,128)(2,1)S(1)}, ...), condition=%wide.region_5.6_spmd.clone, body=%wide.region_4.5_spmd.clone.sunk | while | flops 140357632 | bytes 4489319 | solution.py:49
  79.0 1.9 %fusion.99 = (bf16[4096,128]{1,0:T(8,128)(2,1)S(1)}, bf16[4096,128]{1,0:T(8,128)(2,1)S(1)}) fusion(s32[4096]{0:T(1024)S(1)} %get-tuple-element.183, bf16[4096]{0:T(1024)(128)(2,1)S(1)} %get-tuple-element.184, bf16[4096]{0:T(1024)(128)(2,1)S(1)} %get-tuple-element.185), kind=kLoop, calls=%fused_computation.10.clone.1 | loop fusion | flops 1572864 | bytes 2129920 | tf_op jit(solution)/shard_map/while/body/eval_jaxpr/mul | solution.py:42
  80.9 1.3 fusion.100
  82.4 1.9 %fusion.99 = (bf16[4096,128]{1,0:T(8,128)(2,1)S(1)}, bf16[4096,128]{1,0:T(8,128)(2,1)S(1)}) fusion(s32[4096]{0:T(1024)S(1)} %get-tuple-element.183, bf16[4096]{0:T(1024)(128)(2,1)S(1)} %get-tuple-element.184, bf16[4096]{0:T(1024)(128)(2,1)S(1)} %get-tuple-element.185), kind=kLoop, calls=%fused_computation.10.clone.1 | loop fusion | flops 1572864 | bytes 2129920 | tf_op jit(solution)/shard_map/while/body/eval_jaxpr/mul | solution.py:42
  84.4 1.3 fusion.100
  85.9 1.9 %fusion.99 = (bf16[4096,128]{1,0:T(8,128)(2,1)S(1)}, bf16[4096,128]{1,0:T(8,128)(2,1)S(1)}) fusion(s32[4096]{0:T(1024)S(1)} %get-tuple-element.183, bf16[4096]{0:T(1024)(128)(2,1)S(1)} %get-tuple-element.184, bf16[4096]{0:T(1024)(128)(2,1)S(1)} %get-tuple-element.185), kind=kLoop, calls=%fused_computation.10.clone.1 | loop fusion | flops 1572864 | bytes 2129920 | tf_op jit(solution)/shard_map/while/body/eval_jaxpr/mul | solution.py:42
  87.8 1.3 fusion.100
  89.3 1.9 %fusion.99 = (bf16[4096,128]{1,0:T(8,128)(2,1)S(1)}, bf16[4096,128]{1,0:T(8,128)(2,1)S(1)}) fusion(s32[4096]{0:T(1024)S(1)} %get-tuple-element.183, bf16[4096]{0:T(1024)(128)(2,1)S(1)} %get-tuple-element.184, bf16[4096]{0:T(1024)(128)(2,1)S(1)} %get-tuple-element.185), kind=kLoop, calls=%fused_computation.10.clone.1 | loop fusion | flops 1572864 | bytes 2129920 | tf_op jit(solution)/shard_map/while/body/eval_jaxpr/mul | solution.py:42
  91.3 1.3 fusion.100
  92.8 1.9 %fusion.99 = (bf16[4096,128]{1,0:T(8,128)(2,1)S(1)}, bf16[4096,128]{1,0:T(8,128)(2,1)S(1)}) fusion(s32[4096]{0:T(1024)S(1)} %get-tuple-element.183, bf16[4096]{0:T(1024)(128)(2,1)S(1)} %get-tuple-element.184, bf16[4096]{0:T(1024)(128)(2,1)S(1)} %get-tuple-element.185), kind=kLoop, calls=%fused_computation.10.clone.1 | loop fusion | flops 1572864 | bytes 2129920 | tf_op jit(solution)/shard_map/while/body/eval_jaxpr/mul | solution.py:42
  94.7 1.3 fusion.100
  96.2 1.9 %fusion.99 = (bf16[4096,128]{1,0:T(8,128)(2,1)S(1)}, bf16[4096,128]{1,0:T(8,128)(2,1)S(1)}) fusion(s32[4096]{0:T(1024)S(1)} %get-tuple-element.183, bf16[4096]{0:T(1024)(128)(2,1)S(1)} %get-tuple-element.184, bf16[4096]{0:T(1024)(128)(2,1)S(1)} %get-tuple-element.185), kind=kLoop, calls=%fused_computation.10.clone.1 | loop fusion | flops 1572864 | bytes 2129920 | tf_op jit(solution)/shard_map/while/body/eval_jaxpr/mul | solution.py:42
  98.2 1.3 fusion.100
  99.7 1.9 %fusion.99 = (bf16[4096,128]{1,0:T(8,128)(2,1)S(1)}, bf16[4096,128]{1,0:T(8,128)(2,1)S(1)}) fusion(s32[4096]{0:T(1024)S(1)} %get-tuple-element.183, bf16[4096]{0:T(1024)(128)(2,1)S(1)} %get-tuple-element.184, bf16[4096]{0:T(1024)(128)(2,1)S(1)} %get-tuple-element.185), kind=kLoop, calls=%fused_computation.10.clone.1 | loop fusion | flops 1572864 | bytes 2129920 | tf_op jit(solution)/shard_map/while/body/eval_jaxpr/mul | solution.py:42
  101.6 1.3 fusion.100
  103.1 1.9 %fusion.99 = (bf16[4096,128]{1,0:T(8,128)(2,1)S(1)}, bf16[4096,128]{1,0:T(8,128)(2,1)S(1)}) fusion(s32[4096]{0:T(1024)S(1)} %get-tuple-element.183, bf16[4096]{0:T(1024)(128)(2,1)S(1)} %get-tuple-element.184, bf16[4096]{0:T(1024)(128)(2,1)S(1)} %get-tuple-element.185), kind=kLoop, calls=%fused_computation.10.clone.1 | loop fusion | flops 1572864 | bytes 2129920 | tf_op jit(solution)/shard_map/while/body/eval_jaxpr/mul | solution.py:42
  105.1 1.3 fusion.100
  107.1 45.0 %all-reduce.2.cloned.1.call-done = f32[2,64,128]{2,1,0:T(8,128)} async-done(((f32[2,64,128]{2,1,0:T(8,128)}), f32[2,64,128]{2,1,0:T(8,128)}) %all-reduce.2.cloned.1.call-update) | async-done | bytes 65552 | tf_op jit(solution)/shard_map/psum | solution.py:99
  153.1 5.7 %collective-permute-start = (f32[2,64,2]{2,1,0:T(8,128)S(1)}, f32[2,64,2]{2,1,0:T(8,128)S(1)}, u32[]{:S(2)}, u32[]{:S(2)}) collective-permute-start(f32[2,64,2]{2,1,0:T(8,128)S(1)} %get-tuple-element.142), channel_id=1, source_target_pairs={{0,16},{16,32},{32,48},{48,64},{64,80},{80,96},{96,112},{1,17},{17... | collective-permute-start | bytes 3080 | tf_op jit(solution)/shard_map/ppermute | solution.py:14
  158.8 1.9 %collective-permute-start.1 = (f32[2,64,2]{2,1,0:T(8,128)S(1)}, f32[2,64,2]{2,1,0:T(8,128)S(1)}, u32[]{:S(2)}, u32[]{:S(2)}) collective-permute-start(f32[2,64,2]{2,1,0:T(8,128)S(1)} %get-tuple-element.143), channel_id=1, source_target_pairs={{16,0},{32,16},{48,32},{64,48},{80,64},{96,80},{112,96},{17,1},{33... | collective-permute-start | bytes 3080 | tf_op jit(solution)/shard_map/ppermute | solution.py:15
  161.6 2.8 %collective-permute-done.1 = f32[2,64,2]{2,1,0:T(8,128)S(1)} collective-permute-done((f32[2,64,2]{2,1,0:T(8,128)S(1)}, f32[2,64,2]{2,1,0:T(8,128)S(1)}, u32[]{:S(2)}, u32[]{:S(2)}) %collective-permute-start.1) | collective-permute-done | bytes 1056 | tf_op jit(solution)/shard_map/ppermute | solution.py:15
  165.2 3.2 %collective-permute-start.2 = (f32[2,2,132]{2,1,0:T(2,128)S(1)}, f32[2,2,132]{2,1,0:T(2,128)S(1)}, u32[]{:S(2)}, u32[]{:S(2)}) collective-permute-start(f32[2,2,132]{2,1,0:T(2,128)S(1)} %get-tuple-element.140), channel_id=1, source_target_pairs={{0,1},{1,2},{2,3},{3,4},{4,5},{5,6},{6,7},{7,8},{8,9},{9,10},{10,1... | collective-permute-start | bytes 6344 | tf_op jit(solution)/shard_map/ppermute | solution.py:14
  168.4 1.3 collective-permute-start.3
  169.7 3.0 %collective-permute-done.3 = f32[2,2,132]{2,1,0:T(2,128)S(1)} collective-permute-done((f32[2,2,132]{2,1,0:T(2,128)S(1)}, f32[2,2,132]{2,1,0:T(2,128)S(1)}, u32[]{:S(2)}, u32[]{:S(2)}) %collective-permute-start.3) | collective-permute-done | bytes 2144 | tf_op jit(solution)/shard_map/ppermute | solution.py:15
  172.7 1.1 maximum_maximum_fusion
  173.8 1.0 fusion.92
  (55 shorter events, 9.9 us)
Async XLA Ops:
  11.5 38.6 %all-to-all-start = ((s32[128,2,128]{2,1,0:T(2,128)}), s32[128,2,128]{2,1,0:T(2,128)S(1)}, u32[]{:S(2)}, u32[]{:S(2)}) async-start(s32[128,2,128]{2,1,0:T(2,128)} %bitcast.1), calls=%async_computation | async-start | bytes 262144 | tf_op jit(solution)/shard_map/all_to_all | solution.py:84
  50.1 28.4 %all-to-all-start.1 = ((f32[128,2,2,128]{3,2,1,0:T(2,128)}), f32[128,2,2,128]{3,2,1,0:T(2,128)S(1)}, u32[]{:S(2)}, u32[]{:S(2)}) async-start(f32[128,2,2,128]{3,2,1,0:T(2,128)} %bitcast.4), calls=%async_computation.1 | async-start | bytes 524288 | tf_op jit(solution)/shard_map/all_to_all | solution.py:77
  55.4 96.7 %all-reduce.2.cloned.1.call-start = ((), (), s32[]{:S(2)}) async-start(), calls=%async_computation.2 | async-start | bytes 131072 | tf_op jit(solution)/shard_map/psum | solution.py:99
  106.4 67.4 %copy-start.1 = (f32[64,128]{1,0:T(8,128)S(1)}, f32[64,128]{1,0:T(8,128)}, u32[]{:S(2)}) copy-start(f32[64,128]{1,0:T(8,128)} %param.13) | copy-start | bytes 98308
  152.1 21.7 %copy-start = (f32[2,64,128]{2,1,0:T(8,128)S(1)}, f32[2,64,128]{2,1,0:T(8,128)}, u32[]{:S(2)}) copy-start(f32[2,64,128]{2,1,0:T(8,128)} %all-reduce.2.cloned.1.call-done) | copy-start | bytes 196612
  153.1 8.4 %collective-permute-start = (f32[2,64,2]{2,1,0:T(8,128)S(1)}, f32[2,64,2]{2,1,0:T(8,128)S(1)}, u32[]{:S(2)}, u32[]{:S(2)}) collective-permute-start(f32[2,64,2]{2,1,0:T(8,128)S(1)} %get-tuple-element.142), channel_id=1, source_target_pairs={{0,16},{16,32},{32,48},{48,64},{64,80},{80,96},{96,112},{1,17},{17... | collective-permute-start | bytes 3080 | tf_op jit(solution)/shard_map/ppermute | solution.py:14
  158.8 5.6 %collective-permute-start.1 = (f32[2,64,2]{2,1,0:T(8,128)S(1)}, f32[2,64,2]{2,1,0:T(8,128)S(1)}, u32[]{:S(2)}, u32[]{:S(2)}) collective-permute-start(f32[2,64,2]{2,1,0:T(8,128)S(1)} %get-tuple-element.143), channel_id=1, source_target_pairs={{16,0},{32,16},{48,32},{64,48},{80,64},{96,80},{112,96},{17,1},{33... | collective-permute-start | bytes 3080 | tf_op jit(solution)/shard_map/ppermute | solution.py:15
  165.2 4.5 %collective-permute-start.2 = (f32[2,2,132]{2,1,0:T(2,128)S(1)}, f32[2,2,132]{2,1,0:T(2,128)S(1)}, u32[]{:S(2)}, u32[]{:S(2)}) collective-permute-start(f32[2,2,132]{2,1,0:T(2,128)S(1)} %get-tuple-element.140), channel_id=1, source_target_pairs={{0,1},{1,2},{2,3},{3,4},{4,5},{5,6},{6,7},{7,8},{8,9},{9,10},{10,1... | collective-permute-start | bytes 6344 | tf_op jit(solution)/shard_map/ppermute | solution.py:14
  168.4 4.4 %collective-permute-start.3 = (f32[2,2,132]{2,1,0:T(2,128)S(1)}, f32[2,2,132]{2,1,0:T(2,128)S(1)}, u32[]{:S(2)}, u32[]{:S(2)}) collective-permute-start(f32[2,2,132]{2,1,0:T(2,128)S(1)} %get-tuple-element.141), channel_id=1, source_target_pairs={{1,0},{2,1},{3,2},{4,3},{5,4},{6,5},{7,6},{8,7},{9,8},{10,9},{11,1... | collective-permute-start | bytes 6344 | tf_op jit(solution)/shard_map/ppermute | solution.py:15
Sparse Core Ops, SparseCore 0:
  107.2 44.8 all-reduce.1
where the time goes:
time: 183 us; the launch traced here: 182 us
  waiting for transfers between devices  85.8 us (47%)
  starting transfers between devices  37.8 us (21%)
  other arithmetic  22.5 us (12%)
  between operations  14.3 us (8%)
  matrix products  10.6 us (6%)
  local copies, waits for them, and re-layouts  10.5 us (6%)
    psum x1, waiting for transfers between devices, per_device(): summed = lax.psum(partial_value, 'line')  45 us
    all_to_all x1, waiting for transfers between devices, per_device(): lax.all_to_all(send_vals.reshape(tiles_all, capacity, 2, block_len), ('ti...  22.9 us
    all_to_all x1, starting transfers between devices, per_device(): lax.all_to_all(send_cells.reshape(tiles_all, capacity, block_len), ('tile...  20.4 us
    mul x8, other arithmetic, add_block(): col_hot * block_wz[:, None]  15.4 us
    all_to_all x1, waiting for transfers between devices, per_device(): lax.all_to_all(send_cells.reshape(tiles_all, capacity, block_len), ('tile...  12 us
    dot_general x8, matrix products, add_block(): lax.dot_general(row_hot, right, (((0,), (0,)), ((), ())), preferred_eleme...  10.6 us
    ppermute x2, starting transfers between devices, padded(): before = lax.ppermute(last, axis, up)  8.83 us
    ppermute x2, waiting for transfers between devices, padded(): after = lax.ppermute(initial, axis, down)  5.83 us
  transfers between devices with their start and end apart: 7, of which 5 were waited for; matrix products, arithmetic and copies ran while one was open for 4% of the time, Pallas kernels for 0%

commit v1 on v0

v1 whole, which is shorter than its diff:
```python
import jax
import jax.numpy as jnp
from jax import lax
from jax.experimental import pallas as pl
from jax.experimental.pallas import tpu as pltpu
from jax.sharding import PartitionSpec as P

VMEM_SPEC = pl.BlockSpec(memory_space=pltpu.VMEM)
SMEM_SPEC = pl.BlockSpec(memory_space=pltpu.SMEM)
PARAMS = pltpu.CompilerParams(vmem_limit_bytes=40 * 1024 * 1024)
CAPACITY = 2


def call(kernel, out_shape, specs, cost, scratch=()):
    outs = jax.tree.map(lambda _: VMEM_SPEC, out_shape)
    return pl.pallas_call(
        kernel,
        out_shape=out_shape,
        in_specs=specs,
        out_specs=outs,
        scratch_shapes=list(scratch),
        compiler_params=PARAMS,
        cost_estimate=pl.CostEstimate(flops=cost[0], bytes_accessed=cost[1], transcendentals=0),
    )


def pack_kernel(rows, columns, tile_cols, dest_ref, counts_ref, cells_ref, heights_ref, weights_ref, out_ref):
    blocks = cells_ref.shape[0]
    points = cells_ref.shape[1]
    here = columns * CAPACITY
    slots = rows * here
    dest = dest_ref[...]
    across = jnp.broadcast_to(dest.astype(jnp.float32), (blocks, blocks))
    down = across.T
    before = lax.broadcasted_iota(jnp.int32, (blocks, blocks), 0) < lax.broadcasted_iota(
        jnp.int32, (blocks, blocks), 1
    )
    same = jnp.where((across == down) & before, 1.0, 0.0)
    rank = jnp.sum(same, axis=0, keepdims=True).astype(jnp.int32)
    slot = (dest % rows) * here + (dest // rows) * CAPACITY + rank
    live = lax.broadcasted_iota(jnp.int32, (1, blocks), 1) < counts_ref[0, 0]
    slot = jnp.where(live, slot, slots)
    move = jnp.where(
        lax.broadcasted_iota(jnp.int32, (slots, blocks), 0) == slot, 1.0, 0.0
    ).astype(jnp.bfloat16)
    weights = weights_ref[...]
    cells = cells_ref[...]
    payload = jnp.concatenate(
        [
            (weights * heights_ref[...]).astype(jnp.bfloat16),
            weights.astype(jnp.bfloat16),
            (cells // tile_cols).astype(jnp.float32).astype(jnp.bfloat16),
            (cells % tile_cols).astype(jnp.float32).astype(jnp.bfloat16),
        ],
        axis=1,
    )
    moved = jnp.dot(move, payload, preferred_element_type=jnp.float32)
    out_ref[:, 0:here, :] = moved[:, 0:points].reshape(rows, here, points)
    out_ref[:, here : 2 * here, :] = moved[:, points : 2 * points].reshape(rows, here, points)
    cell = moved[:, 2 * points : 3 * points] * tile_cols + moved[:, 3 * points :]
    out_ref[:, 2 * here :, :] = cell.reshape(rows, here, points)


def bin_kernel(columns, tile_rows, tile_cols, in_ref, sums_ref, top_ref, bottom_ref, row_ref, col_ref):
    sources, held, points = in_ref.shape
    here = held // 3
    cells = in_ref[:, 2 * here :, :].astype(jnp.int32)
    row_ref[...] = (cells // tile_cols).astype(jnp.float32)
    col_ref[...] = (cells % tile_cols).astype(jnp.float32)
    row_ids = lax.broadcasted_iota(jnp.int32, (tile_rows, points), 0).astype(jnp.float32).astype(jnp.bfloat16)
    col_ids = lax.broadcasted_iota(jnp.int32, (tile_cols, points), 0).astype(jnp.float32).astype(jnp.bfloat16)
    zero = jnp.zeros((tile_rows, points), jnp.bfloat16)
    one_col = jnp.ones((tile_cols, points), jnp.bfloat16)
    zero_col = jnp.zeros((tile_cols, points), jnp.bfloat16)

    def spread(ref, source, at, count):
        line = ref[source, pl.ds(at, 1), :]
        return jnp.broadcast_to(line, (count, points)).astype(jnp.bfloat16)

    for column in range(columns):
        total = jnp.zeros((2 * tile_rows, tile_cols), jnp.float32)
        for source in range(0, sources, 2):
            lefts, rights = [], []
            for s in (source, source + 1):
                for k in range(CAPACITY):
                    at = column * CAPACITY + k
                    hit = spread(row_ref, s, at, tile_rows) == row_ids
                    wz = spread(in_ref, s, at, tile_rows)
                    w = spread(in_ref, s, here + at, tile_rows)
                    lefts.append(
                        jnp.concatenate([jnp.where(hit, wz, zero), jnp.where(hit, w, zero)], axis=0)
                    )
                    rights.append(
                        jnp.where(spread(col_ref, s, at, tile_cols) == col_ids, one_col, zero_col)
                    )
            total = total + lax.dot_general(
                jnp.concatenate(lefts, axis=1),
                jnp.concatenate(rights, axis=1),
                (((1,), (1,)), ((), ())),
                preferred_element_type=jnp.float32,
            )
        sums_ref[column] = total
        top_ref[column, 0:2, :] = total[0:2, :]
        top_ref[column, 2:4, :] = total[tile_rows : tile_rows + 2, :]
        bottom_ref[column, 0:2, :] = total[tile_rows - 2 : tile_rows, :]
        bottom_ref[column, 2:4, :] = total[2 * tile_rows - 2 :, :]


def stencil_kernel(lines, sums_ref, above_ref, below_ref, out_ref, held_ref, near_ref, far_ref):
    columns, both, tile_cols = sums_ref.shape
    tile_rows = both // 2
    piece = tile_rows // lines
    tall = tile_rows + 16
    lane = lax.broadcasted_iota(jnp.int32, (tall, tile_cols), 1)
    blank = jnp.zeros((tall, tile_cols), jnp.float32)
    for value in range(2):
        for column in range(columns):
            held_ref[column, 0:8, :] = jnp.zeros((8, tile_cols), jnp.float32)
            held_ref[column, tile_rows + 8 :, :] = jnp.zeros((8, tile_cols), jnp.float32)
            held_ref[column, 8 : tile_rows + 8, :] = sums_ref[
                column, value * tile_rows : (value + 1) * tile_rows, :
            ]
            held_ref[column, 6:8, :] = above_ref[column, 2 * value : 2 * value + 2, :]
            held_ref[column, tile_rows + 8 : tile_rows + 10, :] = below_ref[
                column, 2 * value : 2 * value + 2, :
            ]

        def turned(column):
            if column < 0 or column >= columns:
                return blank, blank, blank, blank
            x = held_ref[column]
            return tuple(pltpu.roll(x, s, 1) for s in (1, 2, tile_cols - 1, tile_cols - 2))

        before, here = turned(-1), turned(0)
        for column in range(columns):
            after = turned(column + 1)
            x = held_ref[column]
            one = jnp.where(lane < 1, before[0], here[0]) + jnp.where(
                lane >= tile_cols - 1, after[2], here[2]
            )
            two = jnp.where(lane < 2, before[1], here[1]) + jnp.where(
                lane >= tile_cols - 2, after[3], here[3]
            )
            same = 2.0 * x + one + 0.25 * two
            near_ref[...] = x + 0.5 * one + 0.2 * two
            far_ref[...] = 0.25 * x + 0.2 * one + 0.125 * two
            out = (
                same[8 : tile_rows + 8, :]
                + near_ref[7 : tile_rows + 7, :]
                + near_ref[9 : tile_rows + 9, :]
                + far_ref[6 : tile_rows + 6, :]
                + far_ref[10 : tile_rows + 10, :]
            )
            for line in range(lines):
                out_ref[line * columns + column, value * piece : (value + 1) * piece, :] = out[
                    line * piece : (line + 1) * piece, :
                ]
            before, here = here, after


def finish_kernel(line_ref, parts_ref, prefire_ref, out_ref):
    sources, both, tile_cols = parts_ref.shape
    lines, piece, _ = out_ref.shape
    total = parts_ref[0]
    for source in range(1, sources):
        total = total + parts_ref[source]
    at = pl.multiple_of(line_ref[0, 0] * piece, piece)
    prefire = prefire_ref[pl.ds(at, piece), :]
    filled = (total[:piece] + 16.0 * prefire) / (total[piece:] + 16.0)
    change = filled - prefire
    for line in range(lines):
        out_ref[line] = change


def per_device(cells, heights, weights, dest, counts, prefire_elevation):
    lines, columns, rows = (lax.axis_size(a) for a in ("line", "tile", "row"))
    blocks, points = cells.shape
    tile_rows, tile_cols = prefire_elevation.shape
    here = columns * CAPACITY
    f32 = jnp.float32
    piece = tile_rows // lines

    packed = call(
        lambda *refs: pack_kernel(rows, columns, tile_cols, *refs),
        jax.ShapeDtypeStruct((rows, 3 * here, points), f32),
        [VMEM_SPEC, SMEM_SPEC, VMEM_SPEC, VMEM_SPEC, VMEM_SPEC],
        (2 * rows * here * blocks * 4 * points, 4 * 6 * rows * here * points),
    )(dest.reshape(1, blocks), counts.reshape(1, 1), cells, heights, weights)
    arrived = lax.all_to_all(packed, "row", split_axis=0, concat_axis=0, tiled=True)

    edge = jax.ShapeDtypeStruct((columns, 4, tile_cols), f32)
    sums, top, bottom = call(
        lambda *refs: bin_kernel(columns, tile_rows, tile_cols, *refs),
        [jax.ShapeDtypeStruct((columns, 2 * tile_rows, tile_cols), f32), edge, edge],
        [VMEM_SPEC],
        (4 * rows * here * points * tile_rows * tile_cols, 4 * 4 * rows * here * points),
        [pltpu.VMEM((rows, here, points), f32), pltpu.VMEM((rows, here, points), f32)],
    )(arrived)
    up = [(i, i + 1) for i in range(rows - 1)]
    above = lax.ppermute(bottom, "row", up)
    below = lax.ppermute(top, "row", [(j, i) for i, j in up])

    tall = tile_rows + 16
    parts = call(
        lambda *refs: stencil_kernel(lines, *refs),
        jax.ShapeDtypeStruct((lines * columns, 2 * piece, tile_cols), f32),
        [VMEM_SPEC] * 3,
        (30 * columns * 2 * tile_rows * tile_cols, 4 * 4 * columns * tile_rows * tile_cols),
        [
            pltpu.VMEM((columns, tall, tile_cols), f32),
            pltpu.VMEM((tall, tile_cols), f32),
            pltpu.VMEM((tall, tile_cols), f32),
        ],
    )(sums, above, below)
    gathered = lax.all_to_all(parts, ("line", "tile"), split_axis=0, concat_axis=0, tiled=True)

    mine = lax.axis_index("line").astype(jnp.int32).reshape(1, 1)
    change = call(
        finish_kernel,
        jax.ShapeDtypeStruct((lines, piece, tile_cols), f32),
        [SMEM_SPEC, VMEM_SPEC, VMEM_SPEC],
        (lines * columns * 2 * piece * tile_cols, 4 * lines * columns * 2 * piece * tile_cols),
    )(mine, gathered, prefire_elevation)
    strips = lax.all_to_all(change, "line", split_axis=0, concat_axis=0, tiled=True)
    return strips.reshape(tile_rows, tile_cols)


def solution(mesh):
    placed = (
        P(("line", "tile", "row"), None),
        P(("line", "tile", "row"), None),
        P(("line", "tile", "row"), None),
        P(("line", "tile", "row")),
        P("line", "tile", "row"),
        P("row", "tile"),
    )
    return jax.shard_map(
        per_device, mesh=mesh, in_specs=placed, out_specs=P("row", "tile"), check_vma=False
    )
```

time: 183 us -> 83.8 us (0.46)
  waiting for transfers between devices: 85.8 us -> 14.7 us
  blocking collectives: 0 us -> 40.2 us
  other arithmetic: 22.5 us -> 0 us
  starting transfers between devices: 37.8 us -> 18.8 us
  between operations: 14.3 us -> 0.72 us
  matrix products: 10.6 us -> 0 us
  local copies, waits for them, and re-layouts: 10.5 us -> 3.78 us
  Pallas kernels: 0 us -> 4.37 us
    psum x1 -> x0, waiting for transfers between devices: 45 us -> none  [per_device(): summed = lax.psum(partial_value, 'line')]
    all_to_all x0 -> x2, blocking collectives: none -> 40.2 us  [the longest x1 33.5 us: per_device(): lax.all_to_all(packed, 'row', split_axis=0, concat_axis=0, tiled=True)]
    all_to_all x2 -> x1, waiting for transfers between devices: 34.9 us -> 11.5 us  [per_device(): lax.all_to_all(parts, ('line', 'tile'), split_axis=0, concat_axis=0, tile...]
    mul x8 -> x0, other arithmetic: 15.4 us -> none  [add_block(): col_hot * block_wz[:, None]]
    all_to_all x2 -> x1, starting transfers between devices: 25.7 us -> 11.2 us  [per_device(): lax.all_to_all(parts, ('line', 'tile'), split_axis=0, concat_axis=0, tile...]
    dot_general x8 -> x0, matrix products: 10.6 us -> none  [add_block(): lax.dot_general(row_hot, right, (((0,), (0,)), ((), ())), preferred_eleme...]
    scatter x2 -> x0, local copies, waits for them, and re-layouts: 5.59 us -> none  [the longest x1 4.4 us: per_device(): send_vals = jnp.zeros((tiles_all * capacity + 1, 2, block_len), jnp.float...]
    ppermute x4 -> x2, starting transfers between devices: 12 us -> 7.56 us  [the longest x1 6.27 us: per_device(): above = lax.ppermute(bottom, 'row', up)]
  transfers between devices with their start and end apart: 7 -> 3, of which waited for: 5 -> 2; matrix products, arithmetic and copies ran while one was open for 4% -> 0% of each run, Pallas kernels for 0% -> 0%
where the time goes in v1:
time: 83.8 us; the launch traced here: 82.6 us
  blocking collectives  40.2 us (48%)
  starting transfers between devices  18.8 us (22%)
  waiting for transfers between devices  14.7 us (18%)
  Pallas kernels  4.37 us (5%)
  local copies, waits for them, and re-layouts  3.78 us (5%)
    all_to_all x1, blocking collectives, per_device(): lax.all_to_all(packed, 'row', split_axis=0, concat_axis=0, tiled=True)  33.5 us
    all_to_all x1, waiting for transfers between devices, per_device(): lax.all_to_all(parts, ('line', 'tile'), split_axis=0, concat_axis=0, tile...  11.5 us
    all_to_all x1, starting transfers between devices, per_device(): lax.all_to_all(parts, ('line', 'tile'), split_axis=0, concat_axis=0, tile...  11.2 us
    all_to_all x1, blocking collectives, per_device(): lax.all_to_all(change, 'line', split_axis=0, concat_axis=0, tiled=True)  6.65 us
    ppermute x1, starting transfers between devices, per_device(): above = lax.ppermute(bottom, 'row', up)  6.27 us
    unnamed x11, local copies, waits for them, and re-layouts  3.78 us
    ppermute x1, waiting for transfers between devices, per_device(): below = lax.ppermute(top, 'row', [(j, i) for i, j in up])  3.17 us
    pallas_call x1, Pallas kernels, per_device(): call(lambda *refs: bin_kernel(columns, tile_rows, tile_cols, *refs), [jax...  2.34 us
  transfers between devices with their start and end apart: 3, of which 2 were waited for; matrix products, arithmetic and copies ran while one was open for 0% of the time, Pallas kernels for 0%

profile of v1, /device:TPU:1, one launch (start us, length us, event | category | flops | bytes accessed | tf_op | source)
XLA Modules:
  0.0 82.6 jit_solution(16066577675579916102)
XLA Ops:
  0.7 0.0 copy-start.4
  0.7 0.6 copy-done.4
  1.3 0.0 copy-start
  1.3 0.8 %copy-done = s32[128,128]{1,0:T(8,128)S(1)} copy-done((s32[128,128]{1,0:T(8,128)S(1)}, s32[128,128]{1,0:T(8,128)}, u32[]{:S(2)}) %copy-start) | copy-done | bytes 65560
  2.1 0.0 copy-start.1
  2.2 0.8 %copy-done.1 = f32[128,128]{1,0:T(8,128)S(1)} copy-done((f32[128,128]{1,0:T(8,128)S(1)}, f32[128,128]{1,0:T(8,128)}, u32[]{:S(2)}) %copy-start.1) | copy-done | bytes 65560
  3.0 0.0 copy-start.2
  3.0 0.8 %copy-done.2 = f32[128,128]{1,0:T(8,128)S(1)} copy-done((f32[128,128]{1,0:T(8,128)S(1)}, f32[128,128]{1,0:T(8,128)}, u32[]{:S(2)}) %copy-start.2) | copy-done | bytes 65560
  3.8 0.3 shard_map.64
  4.1 33.5 %all_to_all.15.refs_0_ = f32[16,48,128]{2,1,0:T(8,128)S(1)} all-to-all(f32[16,48,128]{2,1,0:T(8,128)S(1)} %shard_map.64), channel_id=1, replica_groups=mesh['line'=4,'tile'=8,'row'=16] {'row'}, dimensions={0} | all-to-all | bytes 786432 | tf_op jit(solution)/shard_map/all_to_all | solution.py:189
  37.7 2.3 %shard_map.65 = (f32[8,128,128]{2,1,0:T(8,128)S(1)}, f32[8,4,128]{2,1,0:T(4,128)S(1)}, f32[8,4,128]{2,1,0:T(4,128)S(1)}) custom-call(f32[16,48,128]{2,1,0:T(8,128)S(1)} %all_to_all.15.refs_0_), custom_call_target="tpu_custom_call" | custom-call | flops 1073741824 | bytes 524288 | tf_op jit(solution)/shard_map/pallas_call | solution.py:192
  40.0 6.3 %collective-permute-start = (f32[8,4,128]{2,1,0:T(4,128)S(1)}, f32[8,4,128]{2,1,0:T(4,128)S(1)}, u32[]{:S(2)}, u32[]{:S(2)}) collective-permute-start(f32[8,4,128]{2,1,0:T(4,128)S(1)} %get-tuple-element.9), channel_id=1, source_target_pairs={{0,1},{1,2},{2,3},{3,4},{4,5},{5,6},{6,7},{7,8},{8,9},{9,10},{10,1... | collective-permute-start | bytes 49160 | tf_op jit(solution)/shard_map/ppermute | solution.py:200
  46.3 1.3 %collective-permute-start.1 = (f32[8,4,128]{2,1,0:T(4,128)S(1)}, f32[8,4,128]{2,1,0:T(4,128)S(1)}, u32[]{:S(2)}, u32[]{:S(2)}) collective-permute-start(f32[8,4,128]{2,1,0:T(4,128)S(1)} %get-tuple-element.10), channel_id=1, source_target_pairs={{1,0},{2,1},{3,2},{4,3},{5,4},{6,5},{7,6},{8,7},{9,8},{10,9},{11,1... | collective-permute-start | bytes 49160 | tf_op jit(solution)/shard_map/ppermute | solution.py:201
  47.6 0.0 collective-permute-done.refs_1_
  47.6 3.2 %collective-permute-done.1.refs_2_ = f32[8,4,128]{2,1,0:T(4,128)S(1)} collective-permute-done((f32[8,4,128]{2,1,0:T(4,128)S(1)}, f32[8,4,128]{2,1,0:T(4,128)S(1)}, u32[]{:S(2)}, u32[]{:S(2)}) %collective-permute-start.1) | collective-permute-done | bytes 16416 | tf_op jit(solution)/shard_map/ppermute | solution.py:201
  50.8 1.7 %shard_map.66 = f32[32,32,128]{2,1,0:T(8,128)} custom-call(f32[8,128,128]{2,1,0:T(8,128)S(1)} %get-tuple-element.8.refs_0_, f32[8,4,128]{2,1,0:T(4,128)S(1)} %collective-permute-done.refs_1_, f32[8,4,128]{2,1,0:T(4,128)S(1)} %collective-permute-done.1.refs_2_), custom_call_target="tpu_custom_call" | custom-call | flops 3932160 | bytes 1048576 | tf_op jit(solution)/shard_map/pallas_call | solution.py:204
  52.5 0.0 copy-start.3
  52.5 11.2 %all-to-all-start.1 = ((f32[32,32,128]{2,1,0:T(8,128)}), f32[32,32,128]{2,1,0:T(8,128)S(1)}, u32[]{:S(2)}, u32[]{:S(2)}) async-start(f32[32,32,128]{2,1,0:T(8,128)} %shard_map.66), calls=%async_computation.1 | async-start | bytes 1048576 | tf_op jit(solution)/shard_map/all_to_all | solution.py:215
  63.7 11.5 %all-to-all-done.1.parts_ref = f32[32,32,128]{2,1,0:T(8,128)S(1)} async-done(((f32[32,32,128]{2,1,0:T(8,128)}), f32[32,32,128]{2,1,0:T(8,128)S(1)}, u32[]{:S(2)}, u32[]{:S(2)}) %all-to-all-start.1) | async-done | bytes 524320 | tf_op jit(solution)/shard_map/all_to_all | solution.py:215
  75.2 0.0 copy-done.3
  75.3 6.7 %all_to_all.16 = f32[4,16,128]{2,1,0:T(8,128)S(1)} all-to-all(f32[4,16,128]{2,1,0:T(8,128)S(1)} %shard_map.67), channel_id=1, replica_groups=mesh['line'=4,'tile'=8,'row'=16] {'line'}, dimensions={0} | all-to-all | bytes 65536 | tf_op jit(solution)/shard_map/all_to_all | solution.py:224
  81.9 0.6 copy.9
  (1 shorter events, 0.0 us)
Async XLA Ops:
  0.7 0.7 copy-start.4
  1.3 0.8 %copy-start = (s32[128,128]{1,0:T(8,128)S(1)}, s32[128,128]{1,0:T(8,128)}, u32[]{:S(2)}) copy-start(s32[128,128]{1,0:T(8,128)} %refs_2_.1) | copy-start | bytes 196612
  2.1 0.8 %copy-start.1 = (f32[128,128]{1,0:T(8,128)S(1)}, f32[128,128]{1,0:T(8,128)}, u32[]{:S(2)}) copy-start(f32[128,128]{1,0:T(8,128)} %refs_3_.1) | copy-start | bytes 196612
  3.0 0.8 %copy-start.2 = (f32[128,128]{1,0:T(8,128)S(1)}, f32[128,128]{1,0:T(8,128)}, u32[]{:S(2)}) copy-start(f32[128,128]{1,0:T(8,128)} %refs_4_.1) | copy-start | bytes 196612
  40.0 7.6 %collective-permute-start = (f32[8,4,128]{2,1,0:T(4,128)S(1)}, f32[8,4,128]{2,1,0:T(4,128)S(1)}, u32[]{:S(2)}, u32[]{:S(2)}) collective-permute-start(f32[8,4,128]{2,1,0:T(4,128)S(1)} %get-tuple-element.9), channel_id=1, source_target_pairs={{0,1},{1,2},{2,3},{3,4},{4,5},{5,6},{6,7},{7,8},{8,9},{9,10},{10,1... | collective-permute-start | bytes 49160 | tf_op jit(solution)/shard_map/ppermute | solution.py:200
  46.3 4.5 %collective-permute-start.1 = (f32[8,4,128]{2,1,0:T(4,128)S(1)}, f32[8,4,128]{2,1,0:T(4,128)S(1)}, u32[]{:S(2)}, u32[]{:S(2)}) collective-permute-start(f32[8,4,128]{2,1,0:T(4,128)S(1)} %get-tuple-element.10), channel_id=1, source_target_pairs={{1,0},{2,1},{3,2},{4,3},{5,4},{6,5},{7,6},{8,7},{9,8},{10,9},{11,1... | collective-permute-start | bytes 49160 | tf_op jit(solution)/shard_map/ppermute | solution.py:201
  52.5 22.8 %copy-start.3 = (f32[64,128]{1,0:T(8,128)S(1)}, f32[64,128]{1,0:T(8,128)}, u32[]{:S(2)}) copy-start(f32[64,128]{1,0:T(8,128)} %prefire_ref.1) | copy-start | bytes 98308
  52.5 22.8 %all-to-all-start.1 = ((f32[32,32,128]{2,1,0:T(8,128)}), f32[32,32,128]{2,1,0:T(8,128)S(1)}, u32[]{:S(2)}, u32[]{:S(2)}) async-start(f32[32,32,128]{2,1,0:T(8,128)} %shard_map.66), calls=%async_computation.1 | async-start | bytes 1048576 | tf_op jit(solution)/shard_map/all_to_all | solution.py:215

commit v2 on v1

--- a/solution.py
+++ b/solution.py
@@ -6,12 +6,14 @@
 from jax.sharding import PartitionSpec as P
 
 VMEM_SPEC = pl.BlockSpec(memory_space=pltpu.VMEM)
+HBM_SPEC = pl.BlockSpec(memory_space=pltpu.HBM)
 SMEM_SPEC = pl.BlockSpec(memory_space=pltpu.SMEM)
 PARAMS = pltpu.CompilerParams(vmem_limit_bytes=40 * 1024 * 1024)
+WHOLE_PARAMS = pltpu.CompilerParams(vmem_limit_bytes=60 * 1024 * 1024)
 CAPACITY = 2
 
 
-def call(kernel, out_shape, specs, cost, scratch=()):
+def call(kernel, out_shape, specs, cost, scratch=(), params=PARAMS):
     outs = jax.tree.map(lambda _: VMEM_SPEC, out_shape)
     return pl.pallas_call(
         kernel,
@@ -19,12 +21,28 @@
         in_specs=specs,
         out_specs=outs,
         scratch_shapes=list(scratch),
-        compiler_params=PARAMS,
+        compiler_params=params,
         cost_estimate=pl.CostEstimate(flops=cost[0], bytes_accessed=cost[1], transcendentals=0),
     )
 
 
-def pack_kernel(rows, columns, tile_cols, dest_ref, counts_ref, cells_ref, heights_ref, weights_ref, out_ref):
+def pack_kernel(rows, columns, tile_cols, *refs):
+    dest_hbm, counts_ref, cells_hbm, heights_hbm, weights_hbm, out_ref = refs[:6]
+    dest_ref, cells_ref, heights_ref, weights_ref, sems = refs[6:]
+    copies = [
+        pltpu.make_async_copy(source, target, sems.at[i])
+        for i, (source, target) in enumerate(
+            (
+                (dest_hbm, dest_ref),
+                (weights_hbm, weights_ref),
+                (heights_hbm, heights_ref),
+                (cells_hbm, cells_ref),
+            )
+        )
+    ]
+    for copy in copies:
+        copy.start()
+    copies[0].wait()
     blocks = cells_ref.shape[0]
     points = cells_ref.shape[1]
     here = columns * CAPACITY
@@ -43,6 +61,8 @@
     move = jnp.where(
         lax.broadcasted_iota(jnp.int32, (slots, blocks), 0) == slot, 1.0, 0.0
     ).astype(jnp.bfloat16)
+    for copy in copies[1:]:
+        copy.wait()
     weights = weights_ref[...]
     cells = cells_ref[...]
     payload = jnp.concatenate(
@@ -106,7 +126,7 @@
         bottom_ref[column, 2:4, :] = total[2 * tile_rows - 2 :, :]
 
 
-def stencil_kernel(lines, sums_ref, above_ref, below_ref, out_ref, held_ref, near_ref, far_ref):
+def stencil_kernel(lines, sums_ref, out_ref, held_ref, near_ref, far_ref):
     columns, both, tile_cols = sums_ref.shape
     tile_rows = both // 2
     piece = tile_rows // lines
@@ -120,10 +140,6 @@
             held_ref[column, 8 : tile_rows + 8, :] = sums_ref[
                 column, value * tile_rows : (value + 1) * tile_rows, :
             ]
-            held_ref[column, 6:8, :] = above_ref[column, 2 * value : 2 * value + 2, :]
-            held_ref[column, tile_rows + 8 : tile_rows + 10, :] = below_ref[
-                column, 2 * value : 2 * value + 2, :
-            ]
 
         def turned(column):
             if column < 0 or column >= columns:
@@ -156,6 +172,49 @@
                     line * piece : (line + 1) * piece, :
                 ]
             before, here = here, after
+
+
+def border_kernel(lines, parts_ref, above_ref, below_ref, out_ref):
+    columns, held, tile_cols = above_ref.shape
+    piece = out_ref.shape[1] // 2
+    lane = lax.broadcasted_iota(jnp.int32, (held, tile_cols), 1)
+    blank = jnp.zeros((held, tile_cols), jnp.float32)
+    out_ref[...] = parts_ref[...]
+
+    def filtered(ref):
+        def turned(column):
+            if column < 0 or column >= columns:
+                return blank, blank, blank, blank
+            x = ref[column]
+            return tuple(pltpu.roll(x, s, 1) for s in (1, 2, tile_cols - 1, tile_cols - 2))
+
+        before, here = turned(-1), turned(0)
+        for column in range(columns):
+            after = turned(column + 1)
+            x = ref[column]
+            one = jnp.where(lane < 1, before[0], here[0]) + jnp.where(
+                lane >= tile_cols - 1, after[2], here[2]
+            )
+            two = jnp.where(lane < 2, before[1], here[1]) + jnp.where(
+                lane >= tile_cols - 2, after[3], here[3]
+            )
+            yield column, x + 0.5 * one + 0.2 * two, 0.25 * x + 0.2 * one + 0.125 * two
+            before, here = here, after
+
+    def add(at, row, value):
+        out_ref[at, row : row + 1, :] = parts_ref[at, row : row + 1, :] + value
+
+    for column, near, far in filtered(above_ref):
+        for value in range(2):
+            r = 2 * value
+            add(column, value * piece, far[r : r + 1] + near[r + 1 : r + 2])
+            add(column, value * piece + 1, far[r + 1 : r + 2])
+    last = (lines - 1) * columns
+    for column, near, far in filtered(below_ref):
+        for value in range(2):
+            r = 2 * value
+            add(last + column, (value + 1) * piece - 2, far[r : r + 1])
+            add(last + column, (value + 1) * piece - 1, near[r : r + 1] + far[r + 1 : r + 2])
 
 
 def finish_kernel(line_ref, parts_ref, prefire_ref, out_ref):
@@ -183,8 +242,16 @@
     packed = call(
         lambda *refs: pack_kernel(rows, columns, tile_cols, *refs),
         jax.ShapeDtypeStruct((rows, 3 * here, points), f32),
-        [VMEM_SPEC, SMEM_SPEC, VMEM_SPEC, VMEM_SPEC, VMEM_SPEC],
+        [HBM_SPEC, SMEM_SPEC, HBM_SPEC, HBM_SPEC, HBM_SPEC],
         (2 * rows * here * blocks * 4 * points, 4 * 6 * rows * here * points),
+        [
+            pltpu.VMEM((1, blocks), jnp.int32),
+            pltpu.VMEM((blocks, points), jnp.int32),
+            pltpu.VMEM((blocks, points), f32),
+            pltpu.VMEM((blocks, points), f32),
+            pltpu.SemaphoreType.DMA((4,)),
+        ],
+        params=WHOLE_PARAMS,
     )(dest.reshape(1, blocks), counts.reshape(1, 1), cells, heights, weights)
     arrived = lax.all_to_all(packed, "row", split_axis=0, concat_axis=0, tiled=True)
 
@@ -204,14 +271,20 @@
     parts = call(
         lambda *refs: stencil_kernel(lines, *refs),
         jax.ShapeDtypeStruct((lines * columns, 2 * piece, tile_cols), f32),
-        [VMEM_SPEC] * 3,
-        (30 * columns * 2 * tile_rows * tile_cols, 4 * 4 * columns * tile_rows * tile_cols),
+        [VMEM_SPEC],
+        (60 * columns * 2 * tile_rows * tile_cols, 8 * 4 * columns * tile_rows * tile_cols),
         [
             pltpu.VMEM((columns, tall, tile_cols), f32),
             pltpu.VMEM((tall, tile_cols), f32),
             pltpu.VMEM((tall, tile_cols), f32),
         ],
-    )(sums, above, below)
+    )(sums)
+    parts = call(
+        lambda *refs: border_kernel(lines, *refs),
+        jax.ShapeDtypeStruct((lines * columns, 2 * piece, tile_cols), f32),
+        [VMEM_SPEC] * 3,
+        (30 * columns * 8 * tile_cols, 16 * columns * 8 * tile_cols),
+    )(parts, above, below)
     gathered = lax.all_to_all(parts, ("line", "tile"), split_axis=0, concat_axis=0, tiled=True)
 
     mine = lax.axis_index("line").astype(jnp.int32).reshape(1, 1)

time: 83.8 us -> 81.7 us (0.975)
  local copies, waits for them, and re-layouts: 3.78 us -> 0.62 us
  Pallas kernels: 4.37 us -> 6.06 us
    unnamed x11 -> x3, local copies, waits for them, and re-layouts: 3.78 us -> 0.62 us
    pallas_call x1, Pallas kernels: 0.31 us -> 1.95 us  [per_device(): call(lambda *refs: pack_kernel(rows, columns, tile_cols, *refs), jax.Shap...]
    pallas_call x0 -> x1, Pallas kernels: none -> 0.93 us  [per_device(): call(lambda *refs: border_kernel(lines, *refs), jax.ShapeDtypeStruct((lin...]
    pallas_call x1, Pallas kernels: 1.67 us -> 0.79 us  [per_device(): call(lambda *refs: stencil_kernel(lines, *refs), jax.ShapeDtypeStruct((li...]
  transfers between devices with their start and end apart: 3 -> 3, of which waited for: 2 -> 2; matrix products, arithmetic and copies ran while one was open for 0% -> 0% of each run, Pallas kernels for 0% -> 1%
where the time goes in v2:
time: 81.7 us; the launch traced here: 80.5 us
  blocking collectives  40.4 us (49%)
  starting transfers between devices  18.8 us (23%)
  waiting for transfers between devices  13.9 us (17%)
  Pallas kernels  6.06 us (7%)
    all_to_all x1, blocking collectives, per_device(): lax.all_to_all(packed, 'row', split_axis=0, concat_axis=0, tiled=True)  33.8 us
    all_to_all x1, waiting for transfers between devices, per_device(): lax.all_to_all(parts, ('line', 'tile'), split_axis=0, concat_axis=0, tile...  11.5 us
    all_to_all x1, starting transfers between devices, per_device(): lax.all_to_all(parts, ('line', 'tile'), split_axis=0, concat_axis=0, tile...  11.2 us
    all_to_all x1, blocking collectives, per_device(): lax.all_to_all(change, 'line', split_axis=0, concat_axis=0, tiled=True)  6.65 us
    ppermute x1, starting transfers between devices, per_device(): above = lax.ppermute(bottom, 'row', up)  6.26 us
    ppermute x1, waiting for transfers between devices, per_device(): below = lax.ppermute(top, 'row', [(j, i) for i, j in up])  2.38 us
    pallas_call x1, Pallas kernels, per_device(): call(lambda *refs: bin_kernel(columns, tile_rows, tile_cols, *refs), [jax...  2.34 us
    pallas_call x1, Pallas kernels, per_device(): call(lambda *refs: pack_kernel(rows, columns, tile_cols, *refs), jax.Shap...  1.95 us
  transfers between devices with their start and end apart: 3, of which 2 were waited for; matrix products, arithmetic and copies ran while one was open for 0% of the time, Pallas kernels for 1%

profile of v2, /device:TPU:1, one launch (start us, length us, event | category | flops | bytes accessed | tf_op | source)
XLA Modules:
  0.0 80.5 jit_solution(2032751521943042091)
XLA Ops:
  0.7 2.0 %shard_map.64 = f32[16,48,128]{2,1,0:T(8,128)} custom-call(s32[1,128]{1,0:T(1,128)} %bitcast.6, s32[1,1]{1,0:T(1,128)} %bitcast.4.refs_1_, s32[128,128]{1,0:T(8,128)} %refs_2_.1, f32[128,128]{1,0:T(8,128)} %refs_3_.1, f32[128,128]{1,0:T(8,128)} %refs_4_.1), custom_call_target="tpu_custom_call" | custom-call | flops 33554432 | bytes 786432 | tf_op jit(solution)/shard_map/pallas_call | solution.py:242
  2.6 33.8 %all_to_all.15.refs_0_ = f32[16,48,128]{2,1,0:T(8,128)S(1)} all-to-all(f32[16,48,128]{2,1,0:T(8,128)} %shard_map.64), channel_id=1, replica_groups=mesh['line'=4,'tile'=8,'row'=16] {'row'}, dimensions={0} | all-to-all | bytes 786432 | tf_op jit(solution)/shard_map/all_to_all | solution.py:256
  36.4 2.3 %shard_map.65 = (f32[8,128,128]{2,1,0:T(8,128)S(1)}, f32[8,4,128]{2,1,0:T(4,128)S(1)}, f32[8,4,128]{2,1,0:T(4,128)S(1)}) custom-call(f32[16,48,128]{2,1,0:T(8,128)S(1)} %all_to_all.15.refs_0_), custom_call_target="tpu_custom_call" | custom-call | flops 1073741824 | bytes 524288 | tf_op jit(solution)/shard_map/pallas_call | solution.py:259
  38.7 6.3 %collective-permute-start = (f32[8,4,128]{2,1,0:T(4,128)S(1)}, f32[8,4,128]{2,1,0:T(4,128)S(1)}, u32[]{:S(2)}, u32[]{:S(2)}) collective-permute-start(f32[8,4,128]{2,1,0:T(4,128)S(1)} %get-tuple-element.9), channel_id=1, source_target_pairs={{0,1},{1,2},{2,3},{3,4},{4,5},{5,6},{6,7},{7,8},{8,9},{9,10},{10,1... | collective-permute-start | bytes 49160 | tf_op jit(solution)/shard_map/ppermute | solution.py:267
  45.0 1.3 %collective-permute-start.1 = (f32[8,4,128]{2,1,0:T(4,128)S(1)}, f32[8,4,128]{2,1,0:T(4,128)S(1)}, u32[]{:S(2)}, u32[]{:S(2)}) collective-permute-start(f32[8,4,128]{2,1,0:T(4,128)S(1)} %get-tuple-element.10), channel_id=1, source_target_pairs={{1,0},{2,1},{3,2},{4,3},{5,4},{6,5},{7,6},{8,7},{9,8},{10,9},{11,1... | collective-permute-start | bytes 49160 | tf_op jit(solution)/shard_map/ppermute | solution.py:268
  46.3 0.8 shard_map.66.refs_0_
  47.1 0.0 collective-permute-done.refs_1_
  47.1 2.4 %collective-permute-done.1.refs_2_ = f32[8,4,128]{2,1,0:T(4,128)S(1)} collective-permute-done((f32[8,4,128]{2,1,0:T(4,128)S(1)}, f32[8,4,128]{2,1,0:T(4,128)S(1)}, u32[]{:S(2)}, u32[]{:S(2)}) %collective-permute-start.1) | collective-permute-done | bytes 16416 | tf_op jit(solution)/shard_map/ppermute | solution.py:268
  49.5 0.9 %shard_map.67 = f32[32,32,128]{2,1,0:T(8,128)} custom-call(f32[32,32,128]{2,1,0:T(8,128)S(1)} %shard_map.66.refs_0_, f32[8,4,128]{2,1,0:T(4,128)S(1)} %collective-permute-done.refs_1_, f32[8,4,128]{2,1,0:T(4,128)S(1)} %collective-permute-done.1.refs_2_), custom_call_target="tpu_custom_call" | custom-call | flops 245760 | bytes 131072 | tf_op jit(solution)/shard_map/pallas_call | solution.py:282
  50.4 0.0 copy-start
  50.4 11.2 %all-to-all-start.1 = ((f32[32,32,128]{2,1,0:T(8,128)}), f32[32,32,128]{2,1,0:T(8,128)S(1)}, u32[]{:S(2)}, u32[]{:S(2)}) async-start(f32[32,32,128]{2,1,0:T(8,128)} %shard_map.67), calls=%async_computation.1 | async-start | bytes 1048576 | tf_op jit(solution)/shard_map/all_to_all | solution.py:288
  61.6 11.5 %all-to-all-done.1.parts_ref = f32[32,32,128]{2,1,0:T(8,128)S(1)} async-done(((f32[32,32,128]{2,1,0:T(8,128)}), f32[32,32,128]{2,1,0:T(8,128)S(1)}, u32[]{:S(2)}, u32[]{:S(2)}) %all-to-all-start.1) | async-done | bytes 524320 | tf_op jit(solution)/shard_map/all_to_all | solution.py:288
  73.2 0.0 copy-done
  73.2 6.7 %all_to_all.16 = f32[4,16,128]{2,1,0:T(8,128)S(1)} all-to-all(f32[4,16,128]{2,1,0:T(8,128)S(1)} %shard_map.68), channel_id=1, replica_groups=mesh['line'=4,'tile'=8,'row'=16] {'line'}, dimensions={0} | all-to-all | bytes 65536 | tf_op jit(solution)/shard_map/all_to_all | solution.py:297
  79.9 0.6 copy.9
  (1 shorter events, 0.0 us)
Async XLA Ops:
  38.7 8.4 %collective-permute-start = (f32[8,4,128]{2,1,0:T(4,128)S(1)}, f32[8,4,128]{2,1,0:T(4,128)S(1)}, u32[]{:S(2)}, u32[]{:S(2)}) collective-permute-start(f32[8,4,128]{2,1,0:T(4,128)S(1)} %get-tuple-element.9), channel_id=1, source_target_pairs={{0,1},{1,2},{2,3},{3,4},{4,5},{5,6},{6,7},{7,8},{8,9},{9,10},{10,1... | collective-permute-start | bytes 49160 | tf_op jit(solution)/shard_map/ppermute | solution.py:267
  45.0 4.5 %collective-permute-start.1 = (f32[8,4,128]{2,1,0:T(4,128)S(1)}, f32[8,4,128]{2,1,0:T(4,128)S(1)}, u32[]{:S(2)}, u32[]{:S(2)}) collective-permute-start(f32[8,4,128]{2,1,0:T(4,128)S(1)} %get-tuple-element.10), channel_id=1, source_target_pairs={{1,0},{2,1},{3,2},{4,3},{5,4},{6,5},{7,6},{8,7},{9,8},{10,9},{11,1... | collective-permute-start | bytes 49160 | tf_op jit(solution)/shard_map/ppermute | solution.py:268
  50.4 22.8 %copy-start = (f32[64,128]{1,0:T(8,128)S(1)}, f32[64,128]{1,0:T(8,128)}, u32[]{:S(2)}) copy-start(f32[64,128]{1,0:T(8,128)} %prefire_ref.1) | copy-start | bytes 98308
  50.4 22.8 %all-to-all-start.1 = ((f32[32,32,128]{2,1,0:T(8,128)}), f32[32,32,128]{2,1,0:T(8,128)S(1)}, u32[]{:S(2)}, u32[]{:S(2)}) async-start(f32[32,32,128]{2,1,0:T(8,128)} %shard_map.67), calls=%async_computation.1 | async-start | bytes 1048576 | tf_op jit(solution)/shard_map/all_to_all | solution.py:288

commit v3 on v1

v3 whole, which is shorter than its diff:
```python
import jax
import jax.numpy as jnp
from jax import lax
from jax.experimental import pallas as pl
from jax.experimental.pallas import tpu as pltpu
from jax.sharding import PartitionSpec as P

VMEM_SPEC = pl.BlockSpec(memory_space=pltpu.VMEM)
HBM_SPEC = pl.BlockSpec(memory_space=pltpu.HBM)
SMEM_SPEC = pl.BlockSpec(memory_space=pltpu.SMEM)
PARAMS = pltpu.CompilerParams(vmem_limit_bytes=40 * 1024 * 1024)
WHOLE_PARAMS = pltpu.CompilerParams(vmem_limit_bytes=60 * 1024 * 1024)
CAPACITY = 2


def call(kernel, out_shape, specs, cost, scratch=(), params=PARAMS, out=VMEM_SPEC):
    outs = jax.tree.map(lambda _: out, out_shape)
    return pl.pallas_call(
        kernel,
        out_shape=out_shape,
        in_specs=specs,
        out_specs=outs,
        scratch_shapes=list(scratch),
        compiler_params=params,
        cost_estimate=pl.CostEstimate(flops=cost[0], bytes_accessed=cost[1], transcendentals=0),
    )


def pack_kernel(rows, columns, tile_cols, *refs):
    dest_hbm, counts_ref, cells_hbm, heights_hbm, weights_hbm, out_ref = refs[:6]
    dest_ref, cells_ref, heights_ref, weights_ref, sems = refs[6:]
    copies = [
        pltpu.make_async_copy(source, target, sems.at[i])
        for i, (source, target) in enumerate(
            (
                (dest_hbm, dest_ref),
                (weights_hbm, weights_ref),
                (heights_hbm, heights_ref),
                (cells_hbm, cells_ref),
            )
        )
    ]
    for copy in copies:
        copy.start()
    copies[0].wait()
    blocks = cells_ref.shape[0]
    points = cells_ref.shape[1]
    here = columns * CAPACITY
    slots = rows * here
    dest = dest_ref[...]
    across = jnp.broadcast_to(dest.astype(jnp.float32), (blocks, blocks))
    down = across.T
    before = lax.broadcasted_iota(jnp.int32, (blocks, blocks), 0) < lax.broadcasted_iota(
        jnp.int32, (blocks, blocks), 1
    )
    same = jnp.where((across == down) & before, 1.0, 0.0)
    rank = jnp.sum(same, axis=0, keepdims=True).astype(jnp.int32)
    slot = (dest % rows) * here + (dest // rows) * CAPACITY + rank
    live = lax.broadcasted_iota(jnp.int32, (1, blocks), 1) < counts_ref[0, 0]
    slot = jnp.where(live, slot, slots)
    move = jnp.where(
        lax.broadcasted_iota(jnp.int32, (slots, blocks), 0) == slot, 1.0, 0.0
    ).astype(jnp.bfloat16)
    for copy in copies[1:]:
        copy.wait()
    weights = weights_ref[...]
    cells = cells_ref[...]
    payload = jnp.concatenate(
        [
            (weights * heights_ref[...]).astype(jnp.bfloat16),
            weights.astype(jnp.bfloat16),
            (cells // tile_cols).astype(jnp.float32).astype(jnp.bfloat16),
            (cells % tile_cols).astype(jnp.float32).astype(jnp.bfloat16),
        ],
        axis=1,
    )
    moved = jnp.dot(move, payload, preferred_element_type=jnp.float32)
    out_ref[:, 0:here, :] = moved[:, 0:points].reshape(rows, here, points)
    out_ref[:, here : 2 * here, :] = moved[:, points : 2 * points].reshape(rows, here, points)
    cell = moved[:, 2 * points : 3 * points] * tile_cols + moved[:, 3 * points :]
    out_ref[:, 2 * here :, :] = cell.reshape(rows, here, points)


def strip_kernel(lines, columns, tile_rows, tile_cols, in_ref, out_hbm, *scratch):
    row_ref, col_ref, held_ref, near_ref, far_ref, out_ref, sems = scratch
    sources, held, points = in_ref.shape
    here = held // 3
    piece = tile_rows // lines
    tall = tile_rows + 16
    first, end = 8, 8 + tile_rows
    cells = in_ref[:, 2 * here :, :].astype(jnp.int32)
    row_ref[...] = (cells // tile_cols).astype(jnp.float32)
    col_ref[...] = (cells % tile_cols).astype(jnp.float32)
    row_ids = lax.broadcasted_iota(jnp.int32, (tile_rows, points), 0)
    row_ids = row_ids.astype(jnp.float32).astype(jnp.bfloat16)
    col_ids = lax.broadcasted_iota(jnp.int32, (tile_cols, points), 0)
    col_ids = col_ids.astype(jnp.float32).astype(jnp.bfloat16)
    zero = jnp.zeros((tile_rows, points), jnp.bfloat16)
    one_col = jnp.ones((tile_cols, points), jnp.bfloat16)
    zero_col = jnp.zeros((tile_cols, points), jnp.bfloat16)
    lane = lax.broadcasted_iota(jnp.int32, (tall, tile_cols), 1)
    blank = jnp.zeros((tall, tile_cols), jnp.float32)
    margin = jnp.zeros((8, tile_cols), jnp.float32)

    def spread(ref, source, at, count):
        line = ref[source, pl.ds(at, 1), :]
        return jnp.broadcast_to(line, (count, points)).astype(jnp.bfloat16)

    def add_up(column):
        total = jnp.zeros((2 * tile_rows, tile_cols), jnp.float32)
        for source in range(0, sources, 2):
            lefts, rights = [], []
            for s in (source, source + 1):
                for k in range(CAPACITY):
                    at = column * CAPACITY + k
                    hit = spread(row_ref, s, at, tile_rows) == row_ids
                    wz = spread(in_ref, s, at, tile_rows)
                    w = spread(in_ref, s, here + at, tile_rows)
                    lefts.append(
                        jnp.concatenate([jnp.where(hit, wz, zero), jnp.where(hit, w, zero)], axis=0)
                    )
                    rights.append(
                        jnp.where(spread(col_ref, s, at, tile_cols) == col_ids, one_col, zero_col)
                    )
            total = total + lax.dot_general(
                jnp.concatenate(lefts, axis=1),
                jnp.concatenate(rights, axis=1),
                (((1,), (1,)), ((), ())),
                preferred_element_type=jnp.float32,
            )
        for value in range(2):
            held_ref[value, column, 0:first, :] = margin
            held_ref[value, column, first:end, :] = total[
                value * tile_rows : (value + 1) * tile_rows, :
            ]
            held_ref[value, column, end:, :] = margin

    def turned(value, column):
        if column < 0 or column >= columns:
            return blank, blank, blank, blank
        x = held_ref[value, column]
        return tuple(pltpu.roll(x, s, 1) for s in (1, 2, tile_cols - 1, tile_cols - 2))

    def filter_column(value, column, before, here, after):
        x = held_ref[value, column]
        one = jnp.where(lane < 1, before[0], here[0]) + jnp.where(
            lane >= tile_cols - 1, after[2], here[2]
        )
        two = jnp.where(lane < 2, before[1], here[1]) + jnp.where(
            lane >= tile_cols - 2, after[3], here[3]
        )
        same = 2.0 * x + one + 0.25 * two
        near_ref[value] = x + 0.5 * one + 0.2 * two
        far_ref[value] = 0.25 * x + 0.2 * one + 0.125 * two

        def near(at, count):
            return near_ref[value, at : at + count, :]

        def far(at, count):
            return far_ref[value, at : at + count, :]

        inner = (
            same[first:end, :]
            + near(first - 1, tile_rows)
            + near(first + 1, tile_rows)
            + far(first - 2, tile_rows)
            + far(first + 2, tile_rows)
        )
        outer = jnp.concatenate(
            [
                far(first, 1),
                near(first, 1) + far(first + 1, 1),
                near(end - 1, 1) + far(end - 2, 1),
                far(end - 1, 1),
            ],
            axis=0,
        )
        base = 2 * piece + 2 * value
        for line in range(lines):
            out_ref[line, column, value * piece : (value + 1) * piece, :] = inner[
                line * piece : (line + 1) * piece, :
            ]
            out_ref[line, column, base : base + 2, :] = outer[0:2]
            out_ref[line, column, base + 4 : base + 6, :] = outer[2:4]

    copies = []
    add_up(0)
    before = [turned(value, -1) for value in range(2)]
    here_now = [turned(value, 0) for value in range(2)]
    for column in range(columns):
        if column + 1 < columns:
            add_up(column + 1)
        after = [turned(value, column + 1) for value in range(2)]
        for value in range(2):
            filter_column(value, column, before[value], here_now[value], after[value])
        before, here_now = here_now, after
        copy = pltpu.make_async_copy(out_ref.at[:, column], out_hbm.at[:, column], sems.at[column])
        copy.start()
        copies.append(copy)
    for copy in copies:
        copy.wait()


def gather_kernel(parts_ref, strips_ref, above_ref, below_ref):
    sources = parts_ref.shape[0]
    lines, both, _ = strips_ref.shape
    total = parts_ref[0]
    for source in range(1, sources):
        total = total + parts_ref[source]
    for line in range(lines):
        strips_ref[line] = total[:both]
    above_ref[...] = total[both : both + 4]
    below_ref[...] = total[both + 4 :]


def finish_kernel(strips_ref, top_ref, bottom_ref, prefire_ref, out_ref, wz_ref, w_ref):
    lines, both, _ = strips_ref.shape
    piece = both // 2
    rows = lines * piece
    for value, ref in enumerate((wz_ref, w_ref)):
        for line in range(lines):
            ref[line * piece : (line + 1) * piece, :] = strips_ref[
                line, value * piece : (value + 1) * piece, :
            ]
        ref[0:2, :] = ref[0:2, :] + top_ref[2 * value : 2 * value + 2, :]
        ref[rows - 2 :, :] = ref[rows - 2 :, :] + bottom_ref[2 * value : 2 * value + 2, :]
    prefire = prefire_ref[...]
    filled = (wz_ref[...] + 16.0 * prefire) / (w_ref[...] + 16.0)
    out_ref[...] = filled - prefire


def per_device(cells, heights, weights, dest, counts, prefire_elevation):
    lines, columns, rows = (lax.axis_size(a) for a in ("line", "tile", "row"))
    blocks, points = cells.shape
    tile_rows, tile_cols = prefire_elevation.shape
    here = columns * CAPACITY
    f32 = jnp.float32
    piece = tile_rows // lines

    packed = call(
        lambda *refs: pack_kernel(rows, columns, tile_cols, *refs),
        jax.ShapeDtypeStruct((rows, 3 * here, points), f32),
        [HBM_SPEC, SMEM_SPEC, HBM_SPEC, HBM_SPEC, HBM_SPEC],
        (2 * rows * here * blocks * 4 * points, 4 * 6 * rows * here * points),
        [
            pltpu.VMEM((1, blocks), jnp.int32),
            pltpu.VMEM((blocks, points), jnp.int32),
            pltpu.VMEM((blocks, points), f32),
            pltpu.VMEM((blocks, points), f32),
            pltpu.SemaphoreType.DMA((4,)),
        ],
        params=WHOLE_PARAMS,
    )(dest.reshape(1, blocks), counts.reshape(1, 1), cells, heights, weights)
    arrived = lax.all_to_all(packed, "row", split_axis=0, concat_axis=0, tiled=True)

    tall = tile_rows + 16
    slot = 2 * piece + 8
    parts = call(
        lambda *refs: strip_kernel(lines, columns, tile_rows, tile_cols, *refs),
        jax.ShapeDtypeStruct((lines, columns, slot, tile_cols), f32),
        [VMEM_SPEC],
        (4 * rows * here * points * tile_rows * tile_cols, 4 * 4 * rows * here * points),
        [
            pltpu.VMEM((rows, here, points), f32),
            pltpu.VMEM((rows, here, points), f32),
            pltpu.VMEM((2, columns, tall, tile_cols), f32),
            pltpu.VMEM((2, tall, tile_cols), f32),
            pltpu.VMEM((2, tall, tile_cols), f32),
            pltpu.VMEM((lines, columns, slot, tile_cols), f32),
            pltpu.SemaphoreType.DMA((columns,)),
        ],
        out=HBM_SPEC,
    )(arrived)
    gathered = lax.all_to_all(
        parts.reshape(lines * columns, slot, tile_cols),
        ("line", "tile"),
        split_axis=0,
        concat_axis=0,
        tiled=True,
    )

    edge = jax.ShapeDtypeStruct((4, tile_cols), f32)
    strips, above, below = call(
        gather_kernel,
        [jax.ShapeDtypeStruct((lines, 2 * piece, tile_cols), f32), edge, edge],
        [VMEM_SPEC],
        (lines * columns * slot * tile_cols, 4 * lines * columns * slot * tile_cols),
    )(gathered)
    up = [(i, i + 1) for i in range(rows - 1)]
    top = lax.ppermute(below, "row", up)
    bottom = lax.ppermute(above, "row", [(j, i) for i, j in up])
    strips = lax.all_to_all(strips, "line", split_axis=0, concat_axis=0, tiled=True)

    return call(
        finish_kernel,
        jax.ShapeDtypeStruct((tile_rows, tile_cols), f32),
        [VMEM_SPEC] * 4,
        (8 * tile_rows * tile_cols, 16 * tile_rows * tile_cols),
        [pltpu.VMEM((tile_rows, tile_cols), f32), pltpu.VMEM((tile_rows, tile_cols), f32)],
    )(strips, top, bottom, prefire_elevation)


def solution(mesh):
    placed = (
        P(("line", "tile", "row"), None),
        P(("line", "tile", "row"), None),
        P(("line", "tile", "row"), None),
        P(("line", "tile", "row")),
        P("line", "tile", "row"),
        P("row", "tile"),
    )
    return jax.shard_map(
        per_device, mesh=mesh, in_specs=placed, out_specs=P("row", "tile"), check_vma=False
    )
```

time: 83.8 us -> 82.3 us (0.982)
  the two profiles are of different devices: /device:TPU:1 before, /device:TPU:104 now
where the time goes in v3:
time: 82.3 us; the launch traced here: 81.8 us
  blocking collectives  55.2 us (67%)
  starting transfers between devices  11.9 us (14%)
  Pallas kernels  9.49 us (12%)
  waiting for transfers between devices  4.57 us (6%)
    all_to_all x1, blocking collectives, per_device(): lax.all_to_all(packed, 'row', split_axis=0, concat_axis=0, tiled=True)  37 us
    all_to_all x1, blocking collectives, per_device(): lax.all_to_all(parts.reshape(lines * columns, slot, tile_cols), ('line',...  18.1 us
    pallas_call x1, Pallas kernels, per_device(): call(lambda *refs: strip_kernel(lines, columns, tile_rows, tile_cols, *re...  6.23 us
    all_to_all x1, starting transfers between devices, per_device(): lax.all_to_all(strips, 'line', split_axis=0, concat_axis=0, tiled=True)  6.04 us
    ppermute x1, waiting for transfers between devices, per_device(): bottom = lax.ppermute(above, 'row', [(j, i) for i, j in up])  4.57 us
    ppermute x1, starting transfers between devices, per_device(): top = lax.ppermute(below, 'row', up)  3.73 us
    ppermute x1, starting transfers between devices, per_device(): bottom = lax.ppermute(above, 'row', [(j, i) for i, j in up])  2.1 us
    pallas_call x1, Pallas kernels, per_device(): call(lambda *refs: pack_kernel(rows, columns, tile_cols, *refs), jax.Shap...  1.95 us
  transfers between devices with their start and end apart: 3, of which 1 were waited for; matrix products, arithmetic and copies ran while one was open for 0% of the time, Pallas kernels for 0%

profile of v3, /device:TPU:104, one launch (start us, length us, event | category | flops | bytes accessed | tf_op | source)
XLA Modules:
  0.0 81.8 jit_solution(11069873225821166863)
XLA Ops:
  0.7 2.0 %shard_map.64 = f32[16,48,128]{2,1,0:T(8,128)} custom-call(s32[1,128]{1,0:T(1,128)} %bitcast.5, s32[1,1]{1,0:T(1,128)} %bitcast.3.refs_1_, s32[128,128]{1,0:T(8,128)} %refs_2_.1, f32[128,128]{1,0:T(8,128)} %refs_3_.1, f32[128,128]{1,0:T(8,128)} %refs_4_.1), custom_call_target="tpu_custom_call" | custom-call | flops 33554432 | bytes 786432 | tf_op jit(solution)/shard_map/pallas_call | solution.py:240
  2.6 37.0 %all_to_all.15.refs_0_ = f32[16,48,128]{2,1,0:T(8,128)S(1)} all-to-all(f32[16,48,128]{2,1,0:T(8,128)} %shard_map.64), channel_id=1, replica_groups=mesh['line'=4,'tile'=8,'row'=16] {'row'}, dimensions={0} | all-to-all | bytes 786432 | tf_op jit(solution)/shard_map/all_to_all | solution.py:254
  39.7 6.2 %shard_map.65 = f32[4,8,40,128]{3,2,1,0:T(8,128)S(1)} custom-call(f32[16,48,128]{2,1,0:T(8,128)S(1)} %all_to_all.15.refs_0_), custom_call_target="tpu_custom_call" | custom-call | flops 1073741824 | bytes 524288 | tf_op jit(solution)/shard_map/pallas_call | solution.py:258
  45.9 18.1 %all_to_all.16.parts_ref = f32[32,40,128]{2,1,0:T(8,128)S(1)} all-to-all(f32[32,40,128]{2,1,0:T(8,128)S(1)} %bitcast.4), channel_id=1, replica_groups=mesh['line'=4,'tile'=8,'row'=16] {'line','tile'}, dimensions={0} | all-to-all | bytes 1310720 | tf_op jit(solution)/shard_map/all_to_all | solution.py:274
  64.0 0.7 shard_map.66
  64.7 0.0 copy-start
  64.7 6.0 %all-to-all-start.2 = ((f32[4,32,128]{2,1,0:T(8,128)}), f32[4,32,128]{2,1,0:T(8,128)S(1)}, u32[]{:S(2)}, u32[]{:S(2)}) async-start(f32[4,32,128]{2,1,0:T(8,128)} %get-tuple-element.8), calls=%async_computation.2 | async-start | bytes 131072 | tf_op jit(solution)/shard_map/all_to_all | solution.py:292
  70.7 3.7 %collective-permute-start = (f32[4,128]{1,0:T(4,128)S(1)}, f32[4,128]{1,0:T(4,128)S(1)}, u32[]{:S(2)}, u32[]{:S(2)}) collective-permute-start(f32[4,128]{1,0:T(4,128)S(1)} %get-tuple-element.9), channel_id=1, source_target_pairs={{0,1},{1,2},{2,3},{3,4},{4,5},{5,6},{6,7},{7,8},{8,9},{9,10},{10,1... | collective-permute-start | bytes 6152 | tf_op jit(solution)/shard_map/ppermute | solution.py:290
  74.5 2.1 %collective-permute-start.1 = (f32[4,128]{1,0:T(4,128)S(1)}, f32[4,128]{1,0:T(4,128)S(1)}, u32[]{:S(2)}, u32[]{:S(2)}) collective-permute-start(f32[4,128]{1,0:T(4,128)S(1)} %get-tuple-element.10), channel_id=1, source_target_pairs={{1,0},{2,1},{3,2},{4,3},{5,4},{6,5},{7,6},{8,7},{9,8},{10,9},{11,1... | collective-permute-start | bytes 6152 | tf_op jit(solution)/shard_map/ppermute | solution.py:291
  76.6 0.0 collective-permute-done.top_ref
  76.6 4.6 %collective-permute-done.1.bottom_ref = f32[4,128]{1,0:T(4,128)S(1)} collective-permute-done((f32[4,128]{1,0:T(4,128)S(1)}, f32[4,128]{1,0:T(4,128)S(1)}, u32[]{:S(2)}, u32[]{:S(2)}) %collective-permute-start.1) | collective-permute-done | bytes 2080 | tf_op jit(solution)/shard_map/ppermute | solution.py:291
  81.2 0.0 all-to-all-done.2.strips_ref
  81.2 0.0 copy-done
  81.2 0.6 shard_map.67
Async XLA Ops:
  64.7 16.5 %copy-start = (f32[64,128]{1,0:T(8,128)S(1)}, f32[64,128]{1,0:T(8,128)}, u32[]{:S(2)}) copy-start(f32[64,128]{1,0:T(8,128)} %prefire_ref.1) | copy-start | bytes 98308
  64.7 16.5 %all-to-all-start.2 = ((f32[4,32,128]{2,1,0:T(8,128)}), f32[4,32,128]{2,1,0:T(8,128)S(1)}, u32[]{:S(2)}, u32[]{:S(2)}) async-start(f32[4,32,128]{2,1,0:T(8,128)} %get-tuple-element.8), calls=%async_computation.2 | async-start | bytes 131072 | tf_op jit(solution)/shard_map/all_to_all | solution.py:292
  70.7 5.8 %collective-permute-start = (f32[4,128]{1,0:T(4,128)S(1)}, f32[4,128]{1,0:T(4,128)S(1)}, u32[]{:S(2)}, u32[]{:S(2)}) collective-permute-start(f32[4,128]{1,0:T(4,128)S(1)} %get-tuple-element.9), channel_id=1, source_target_pairs={{0,1},{1,2},{2,3},{3,4},{4,5},{5,6},{6,7},{7,8},{8,9},{9,10},{10,1... | collective-permute-start | bytes 6152 | tf_op jit(solution)/shard_map/ppermute | solution.py:290
  74.5 6.7 %collective-permute-start.1 = (f32[4,128]{1,0:T(4,128)S(1)}, f32[4,128]{1,0:T(4,128)S(1)}, u32[]{:S(2)}, u32[]{:S(2)}) collective-permute-start(f32[4,128]{1,0:T(4,128)S(1)} %get-tuple-element.10), channel_id=1, source_target_pairs={{1,0},{2,1},{3,2},{4,3},{5,4},{6,5},{7,6},{8,7},{9,8},{10,9},{11,1... | collective-permute-start | bytes 6152 | tf_op jit(solution)/shard_map/ppermute | solution.py:291

commit v4 on v3

--- a/solution.py
+++ b/solution.py
@@ -3,6 +3,7 @@
 from jax import lax
 from jax.experimental import pallas as pl
 from jax.experimental.pallas import tpu as pltpu
+from jax.sharding import Mesh
 from jax.sharding import PartitionSpec as P
 
 VMEM_SPEC = pl.BlockSpec(memory_space=pltpu.VMEM)
@@ -11,6 +12,7 @@
 PARAMS = pltpu.CompilerParams(vmem_limit_bytes=40 * 1024 * 1024)
 WHOLE_PARAMS = pltpu.CompilerParams(vmem_limit_bytes=60 * 1024 * 1024)
 CAPACITY = 2
+ROW = ("pair", "side")
 
 
 def call(kernel, out_shape, specs, cost, scratch=(), params=PARAMS, out=VMEM_SPEC):
@@ -183,7 +185,6 @@
             out_ref[line, column, base : base + 2, :] = outer[0:2]
             out_ref[line, column, base + 4 : base + 6, :] = outer[2:4]
 
-    copies = []
     add_up(0)
     before = [turned(value, -1) for value in range(2)]
     here_now = [turned(value, 0) for value in range(2)]
@@ -194,43 +195,54 @@
         for value in range(2):
             filter_column(value, column, before[value], here_now[value], after[value])
         before, here_now = here_now, after
-        copy = pltpu.make_async_copy(out_ref.at[:, column], out_hbm.at[:, column], sems.at[column])
-        copy.start()
-        copies.append(copy)
-    for copy in copies:
-        copy.wait()
-
-
-def gather_kernel(parts_ref, strips_ref, above_ref, below_ref):
+    copy = pltpu.make_async_copy(out_ref, out_hbm, sems.at[0])
+    copy.start()
+    copy.wait()
+
+
+def gather_kernel(side_ref, parts_ref, strips_ref, cross_ref):
     sources = parts_ref.shape[0]
-    lines, both, _ = strips_ref.shape
+    ends, both, tile_cols = strips_ref.shape
     total = parts_ref[0]
     for source in range(1, sources):
         total = total + parts_ref[source]
-    for line in range(lines):
-        strips_ref[line] = total[:both]
-    above_ref[...] = total[both : both + 4]
-    below_ref[...] = total[both + 4 :]
-
-
-def finish_kernel(strips_ref, top_ref, bottom_ref, prefire_ref, out_ref, wz_ref, w_ref):
-    lines, both, _ = strips_ref.shape
+    above = total[both : both + 4]
+    below = total[both + 4 :]
+    side = side_ref[0, 0]
+    lower = side == 0
+    partner = jnp.concatenate(
+        [jnp.where(lower, below, above), jnp.zeros((both - 4, tile_cols), jnp.float32)], axis=0
+    )
+    for line in range(ends // 2):
+        strips_ref[2 * line + side] = total[:both]
+        strips_ref[2 * line + 1 - side] = partner
+    cross_ref[...] = jnp.where(lower, above, below)
+
+
+def finish_kernel(side_ref, strips_ref, cross_ref, prefire_ref, out_ref, wz_ref, w_ref):
+    ends, both, _ = strips_ref.shape
+    lines = ends // 2
     piece = both // 2
     rows = lines * piece
+    side = side_ref[0, 0]
+    partner = strips_ref[1 - side, 0:4, :]
+    cross = cross_ref[...]
+    top = jnp.where(side == 0, cross, partner)
+    bottom = jnp.where(side == 0, partner, cross)
     for value, ref in enumerate((wz_ref, w_ref)):
         for line in range(lines):
             ref[line * piece : (line + 1) * piece, :] = strips_ref[
-                line, value * piece : (value + 1) * piece, :
+                2 * line + side, value * piece : (value + 1) * piece, :
             ]
-        ref[0:2, :] = ref[0:2, :] + top_ref[2 * value : 2 * value + 2, :]
-        ref[rows - 2 :, :] = ref[rows - 2 :, :] + bottom_ref[2 * value : 2 * value + 2, :]
+        ref[0:2, :] = ref[0:2, :] + top[2 * value : 2 * value + 2]
+        ref[rows - 2 :, :] = ref[rows - 2 :, :] + bottom[2 * value : 2 * value + 2]
     prefire = prefire_ref[...]
     filled = (wz_ref[...] + 16.0 * prefire) / (w_ref[...] + 16.0)
     out_ref[...] = filled - prefire
 
 
 def per_device(cells, heights, weights, dest, counts, prefire_elevation):
-    lines, columns, rows = (lax.axis_size(a) for a in ("line", "tile", "row"))
+    lines, columns, rows = (lax.axis_size(a) for a in ("line", "tile", ROW))
     blocks, points = cells.shape
     tile_rows, tile_cols = prefire_elevation.shape
     here = columns * CAPACITY
@@ -251,7 +263,7 @@
         ],
         params=WHOLE_PARAMS,
     )(dest.reshape(1, blocks), counts.reshape(1, 1), cells, heights, weights)
-    arrived = lax.all_to_all(packed, "row", split_axis=0, concat_axis=0, tiled=True)
+    arrived = lax.all_to_all(packed, ROW, split_axis=0, concat_axis=0, tiled=True)
 
     tall = tile_rows + 16
     slot = 2 * piece + 8
@@ -267,7 +279,7 @@
             pltpu.VMEM((2, tall, tile_cols), f32),
             pltpu.VMEM((2, tall, tile_cols), f32),
             pltpu.VMEM((lines, columns, slot, tile_cols), f32),
-            pltpu.SemaphoreType.DMA((columns,)),
+            pltpu.SemaphoreType.DMA((1,)),
         ],
         out=HBM_SPEC,
     )(arrived)
@@ -279,36 +291,42 @@
         tiled=True,
     )
 
-    edge = jax.ShapeDtypeStruct((4, tile_cols), f32)
-    strips, above, below = call(
+    side = lax.axis_index("side").astype(jnp.int32).reshape(1, 1)
+    strips, cross = call(
         gather_kernel,
-        [jax.ShapeDtypeStruct((lines, 2 * piece, tile_cols), f32), edge, edge],
-        [VMEM_SPEC],
+        [
+            jax.ShapeDtypeStruct((2 * lines, 2 * piece, tile_cols), f32),
+            jax.ShapeDtypeStruct((4, tile_cols), f32),
+        ],
+        [SMEM_SPEC, VMEM_SPEC],
         (lines * columns * slot * tile_cols, 4 * lines * columns * slot * tile_cols),
-    )(gathered)
-    up = [(i, i + 1) for i in range(rows - 1)]
-    top = lax.ppermute(below, "row", up)
-    bottom = lax.ppermute(above, "row", [(j, i) for i, j in up])
-    strips = lax.all_to_all(strips, "line", split_axis=0, concat_axis=0, tiled=True)
+    )(side, gathered)
+    swap = [(i, i + 1) for i in range(1, rows - 1, 2)]
+    cross = lax.ppermute(cross, ROW, swap + [(j, i) for i, j in swap])
+    strips = lax.all_to_all(strips, ("line", "side"), split_axis=0, concat_axis=0, tiled=True)
 
     return call(
         finish_kernel,
         jax.ShapeDtypeStruct((tile_rows, tile_cols), f32),
-        [VMEM_SPEC] * 4,
+        [SMEM_SPEC] + [VMEM_SPEC] * 3,
         (8 * tile_rows * tile_cols, 16 * tile_rows * tile_cols),
         [pltpu.VMEM((tile_rows, tile_cols), f32), pltpu.VMEM((tile_rows, tile_cols), f32)],
-    )(strips, top, bottom, prefire_elevation)
+    )(side, strips, cross, prefire_elevation)
 
 
 def solution(mesh):
+    lines, columns, rows = (mesh.shape[a] for a in ("line", "tile", "row"))
+    paired = Mesh(
+        mesh.devices.reshape(lines, columns, rows // 2, 2), ("line", "tile", "pair", "side")
+    )
     placed = (
-        P(("line", "tile", "row"), None),
-        P(("line", "tile", "row"), None),
-        P(("line", "tile", "row"), None),
-        P(("line", "tile", "row")),
-        P("line", "tile", "row"),
-        P("row", "tile"),
+        P(("line", "tile") + ROW, None),
+        P(("line", "tile") + ROW, None),
+        P(("line", "tile") + ROW, None),
+        P(("line", "tile") + ROW),
+        P("line", "tile", ROW),
+        P(ROW, "tile"),
     )
     return jax.shard_map(
-        per_device, mesh=mesh, in_specs=placed, out_specs=P("row", "tile"), check_vma=False
-    )
+        per_device, mesh=paired, in_specs=placed, out_specs=P(ROW, "tile"), check_vma=False
+    )

time: 82.3 us -> 77.7 us (0.944)
  the two profiles are of different devices: /device:TPU:104 before, /device:TPU:1 now
where the time goes in v4:
time: 77.7 us; the launch traced here: 77.2 us
  blocking collectives  33.8 us (44%)
  starting transfers between devices  18 us (23%)
  waiting for transfers between devices  17.8 us (23%)
  Pallas kernels  7 us (9%)
    all_to_all x1, blocking collectives, per_device(): lax.all_to_all(packed, ROW, split_axis=0, concat_axis=0, tiled=True)  33.8 us
    all_to_all x1, starting transfers between devices, per_device(): lax.all_to_all(parts.reshape(lines * columns, slot, tile_cols), ('line',...  13.8 us
    all_to_all x1, waiting for transfers between devices, per_device(): lax.all_to_all(parts.reshape(lines * columns, slot, tile_cols), ('line',...  12.9 us
    all_to_all x1, waiting for transfers between devices, per_device(): lax.all_to_all(strips, ('line', 'side'), split_axis=0, concat_axis=0, til...  4.85 us
    pallas_call x1, Pallas kernels, per_device(): call(lambda *refs: strip_kernel(lines, columns, tile_rows, tile_cols, *re...  3.68 us
    all_to_all x1, starting transfers between devices, per_device(): lax.all_to_all(strips, ('line', 'side'), split_axis=0, concat_axis=0, til...  3.5 us
    pallas_call x1, Pallas kernels, per_device(): call(lambda *refs: pack_kernel(rows, columns, tile_cols, *refs), jax.Shap...  1.97 us
  transfers between devices with their start and end apart: 3, of which 2 were waited for; matrix products, arithmetic and copies ran while one was open for 0% of the time, Pallas kernels for 0%

profile of v4, /device:TPU:1, one launch (start us, length us, event | category | flops | bytes accessed | tf_op | source)
XLA Modules:
  0.0 77.2 jit_solution(7204674971890275339)
XLA Ops:
  0.7 2.0 %shard_map.64 = f32[16,48,128]{2,1,0:T(8,128)} custom-call(s32[1,128]{1,0:T(1,128)} %bitcast.5, s32[1,1]{1,0:T(1,128)} %bitcast.4.refs_1_, s32[128,128]{1,0:T(8,128)} %refs_2_.1, f32[128,128]{1,0:T(8,128)} %refs_3_.1, f32[128,128]{1,0:T(8,128)} %refs_4_.1), custom_call_target="tpu_custom_call" | custom-call | flops 33554432 | bytes 786432 | tf_op jit(solution)/shard_map/pallas_call | solution.py:252
  2.6 33.8 %all_to_all.15.refs_0_ = f32[16,48,128]{2,1,0:T(8,128)S(1)} all-to-all(f32[16,48,128]{2,1,0:T(8,128)} %shard_map.64), channel_id=1, replica_groups=mesh['line'=4,'tile'=8,'pair'=8,'side'=2] {'pair','side'}, dimensions={0} | all-to-all | bytes 786432 | tf_op jit(solution)/shard_map/all_to_all | solution.py:266
  36.4 3.7 %shard_map.65 = f32[4,8,40,128]{3,2,1,0:T(8,128)} custom-call(f32[16,48,128]{2,1,0:T(8,128)S(1)} %all_to_all.15.refs_0_), custom_call_target="tpu_custom_call" | custom-call | flops 1073741824 | bytes 524288 | tf_op jit(solution)/shard_map/pallas_call | solution.py:270
  40.1 13.8 %all-to-all-start.1 = ((f32[32,40,128]{2,1,0:T(8,128)}), f32[32,40,128]{2,1,0:T(8,128)S(1)}, u32[]{:S(2)}, u32[]{:S(2)}) async-start(f32[32,40,128]{2,1,0:T(8,128)} %bitcast.3), calls=%async_computation.1 | async-start | bytes 1310720 | tf_op jit(solution)/shard_map/all_to_all | solution.py:286
  53.9 12.9 %all-to-all-done.1.parts_ref = f32[32,40,128]{2,1,0:T(8,128)S(1)} async-done(((f32[32,40,128]{2,1,0:T(8,128)}), f32[32,40,128]{2,1,0:T(8,128)S(1)}, u32[]{:S(2)}, u32[]{:S(2)}) %all-to-all-start.1) | async-done | bytes 655392 | tf_op jit(solution)/shard_map/all_to_all | solution.py:286
  66.8 0.7 shard_map.66
  67.5 0.0 copy-start
  67.5 3.5 %all-to-all-start.2 = ((f32[8,32,128]{2,1,0:T(8,128)}), f32[8,32,128]{2,1,0:T(8,128)S(1)}, u32[]{:S(2)}, u32[]{:S(2)}) async-start(f32[8,32,128]{2,1,0:T(8,128)} %get-tuple-element.7), calls=%async_computation.2 | async-start | bytes 262144 | tf_op jit(solution)/shard_map/all_to_all | solution.py:306
  71.0 0.7 collective-permute-start
  71.7 0.0 collective-permute-done.cross_ref
  71.7 4.9 %all-to-all-done.2.strips_ref = f32[8,32,128]{2,1,0:T(8,128)S(1)} async-done(((f32[8,32,128]{2,1,0:T(8,128)}), f32[8,32,128]{2,1,0:T(8,128)S(1)}, u32[]{:S(2)}, u32[]{:S(2)}) %all-to-all-start.2) | async-done | bytes 131104 | tf_op jit(solution)/shard_map/all_to_all | solution.py:306
  76.6 0.0 copy-done
  76.6 0.6 shard_map.67
Async XLA Ops:
  40.1 26.7 %all-to-all-start.1 = ((f32[32,40,128]{2,1,0:T(8,128)}), f32[32,40,128]{2,1,0:T(8,128)S(1)}, u32[]{:S(2)}, u32[]{:S(2)}) async-start(f32[32,40,128]{2,1,0:T(8,128)} %bitcast.3), calls=%async_computation.1 | async-start | bytes 1310720 | tf_op jit(solution)/shard_map/all_to_all | solution.py:286
  67.5 9.0 %copy-start = (f32[64,128]{1,0:T(8,128)S(1)}, f32[64,128]{1,0:T(8,128)}, u32[]{:S(2)}) copy-start(f32[64,128]{1,0:T(8,128)} %prefire_ref.1) | copy-start | bytes 98308
  67.5 9.0 %all-to-all-start.2 = ((f32[8,32,128]{2,1,0:T(8,128)}), f32[8,32,128]{2,1,0:T(8,128)S(1)}, u32[]{:S(2)}, u32[]{:S(2)}) async-start(f32[8,32,128]{2,1,0:T(8,128)} %get-tuple-element.7), calls=%async_computation.2 | async-start | bytes 262144 | tf_op jit(solution)/shard_map/all_to_all | solution.py:306
  71.0 0.7 collective-permute-start

commit v5 on v4

--- a/solution.py
+++ b/solution.py
@@ -13,10 +13,34 @@
 WHOLE_PARAMS = pltpu.CompilerParams(vmem_limit_bytes=60 * 1024 * 1024)
 CAPACITY = 2
 ROW = ("pair", "side")
-
-
-def call(kernel, out_shape, specs, cost, scratch=(), params=PARAMS, out=VMEM_SPEC):
-    outs = jax.tree.map(lambda _: out, out_shape)
+EVERY = ("line", "tile") + ROW
+ROW_ORDER = [10, 0, 5, 11, 13, 6, 3, 14, 4, 12, 2, 9, 7, 15, 1, 8]
+STRIP_ORDER = [27, 11, 0, 13, 29, 25, 31, 18, 17, 10, 5, 3, 4, 1, 15, 26, 12, 30, 21, 14, 2, 9, 28, 23, 8, 7, 16, 20, 24, 22, 19, 6]
+END_ORDER = [0, 1, 2, 3, 4, 5, 6, 7]
+
+
+def row_groups(lines, columns, rows):
+    return [
+        [(a * columns + b) * rows + z for z in ROW_ORDER]
+        for a in range(lines)
+        for b in range(columns)
+    ]
+
+
+def strip_groups(columns, rows):
+    return [[m * rows + z for m in STRIP_ORDER] for z in range(rows)]
+
+
+def end_groups(columns, rows):
+    return [
+        [(m // 2 * columns + b) * rows + 2 * p + m % 2 for m in END_ORDER]
+        for b in range(columns)
+        for p in range(rows // 2)
+    ]
+
+
+def call(kernel, out_shape, specs, cost, scratch=(), params=PARAMS):
+    outs = jax.tree.map(lambda _: VMEM_SPEC, out_shape)
     return pl.pallas_call(
         kernel,
         out_shape=out_shape,
@@ -29,8 +53,8 @@
 
 
 def pack_kernel(rows, columns, tile_cols, *refs):
-    dest_hbm, counts_ref, cells_hbm, heights_hbm, weights_hbm, out_ref = refs[:6]
-    dest_ref, cells_ref, heights_ref, weights_ref, sems = refs[6:]
+    _, dest_hbm, counts_ref, cells_hbm, heights_hbm, weights_hbm, out_ref = refs[:7]
+    dest_ref, cells_ref, heights_ref, weights_ref, sems = refs[7:]
     copies = [
         pltpu.make_async_copy(source, target, sems.at[i])
         for i, (source, target) in enumerate(
@@ -57,7 +81,11 @@
     )
     same = jnp.where((across == down) & before, 1.0, 0.0)
     rank = jnp.sum(same, axis=0, keepdims=True).astype(jnp.int32)
-    slot = (dest % rows) * here + (dest // rows) * CAPACITY + rank
+    tile_row = dest % rows
+    place = tile_row
+    for position, row in enumerate(ROW_ORDER):
+        place = jnp.where(tile_row == row, position, place)
+    slot = place * here + (dest // rows) * CAPACITY + rank
     live = lax.broadcasted_iota(jnp.int32, (1, blocks), 1) < counts_ref[0, 0]
     slot = jnp.where(live, slot, slots)
     move = jnp.where(
@@ -83,8 +111,8 @@
     out_ref[:, 2 * here :, :] = cell.reshape(rows, here, points)
 
 
-def strip_kernel(lines, columns, tile_rows, tile_cols, in_ref, out_hbm, *scratch):
-    row_ref, col_ref, held_ref, near_ref, far_ref, out_ref, sems = scratch
+def strip_kernel(lines, columns, tile_rows, tile_cols, in_ref, out_ref, *scratch):
+    row_ref, col_ref, held_ref, near_ref, far_ref = scratch
     sources, held, points = in_ref.shape
     here = held // 3
     piece = tile_rows // lines
@@ -179,11 +207,12 @@
         )
         base = 2 * piece + 2 * value
         for line in range(lines):
-            out_ref[line, column, value * piece : (value + 1) * piece, :] = inner[
+            at = STRIP_ORDER.index(line * columns + column)
+            out_ref[at, value * piece : (value + 1) * piece, :] = inner[
                 line * piece : (line + 1) * piece, :
             ]
-            out_ref[line, column, base : base + 2, :] = outer[0:2]
-            out_ref[line, column, base + 4 : base + 6, :] = outer[2:4]
+            out_ref[at, base : base + 2, :] = outer[0:2]
+            out_ref[at, base + 4 : base + 6, :] = outer[2:4]
 
     add_up(0)
     before = [turned(value, -1) for value in range(2)]
@@ -195,9 +224,11 @@
         for value in range(2):
             filter_column(value, column, before[value], here_now[value], after[value])
         before, here_now = here_now, after
-    copy = pltpu.make_async_copy(out_ref, out_hbm, sems.at[0])
-    copy.start()
-    copy.wait()
+
+
+def end_places(line, side):
+    lower, upper = END_ORDER.index(2 * line), END_ORDER.index(2 * line + 1)
+    return jnp.where(side == 0, lower, upper), jnp.where(side == 0, upper, lower)
 
 
 def gather_kernel(side_ref, parts_ref, strips_ref, cross_ref):
@@ -214,8 +245,9 @@
         [jnp.where(lower, below, above), jnp.zeros((both - 4, tile_cols), jnp.float32)], axis=0
     )
     for line in range(ends // 2):
-        strips_ref[2 * line + side] = total[:both]
-        strips_ref[2 * line + 1 - side] = partner
+        here, there = end_places(line, side)
+        strips_ref[here] = total[:both]
+        strips_ref[there] = partner
     cross_ref[...] = jnp.where(lower, above, below)
 
 
@@ -225,14 +257,14 @@
     piece = both // 2
     rows = lines * piece
     side = side_ref[0, 0]
-    partner = strips_ref[1 - side, 0:4, :]
+    partner = strips_ref[end_places(0, side)[1], 0:4, :]
     cross = cross_ref[...]
     top = jnp.where(side == 0, cross, partner)
     bottom = jnp.where(side == 0, partner, cross)
     for value, ref in enumerate((wz_ref, w_ref)):
         for line in range(lines):
             ref[line * piece : (line + 1) * piece, :] = strips_ref[
-                2 * line + side, value * piece : (value + 1) * piece, :
+                end_places(line, side)[0], value * piece : (value + 1) * piece, :
             ]
         ref[0:2, :] = ref[0:2, :] + top[2 * value : 2 * value + 2]
         ref[rows - 2 :, :] = ref[rows - 2 :, :] + bottom[2 * value : 2 * value + 2]
@@ -249,10 +281,11 @@
     f32 = jnp.float32
     piece = tile_rows // lines
 
+    side = lax.axis_index("side").astype(jnp.int32).reshape(1, 1)
     packed = call(
         lambda *refs: pack_kernel(rows, columns, tile_cols, *refs),
         jax.ShapeDtypeStruct((rows, 3 * here, points), f32),
-        [HBM_SPEC, SMEM_SPEC, HBM_SPEC, HBM_SPEC, HBM_SPEC],
+        [SMEM_SPEC, HBM_SPEC, SMEM_SPEC, HBM_SPEC, HBM_SPEC, HBM_SPEC],
         (2 * rows * here * blocks * 4 * points, 4 * 6 * rows * here * points),
         [
             pltpu.VMEM((1, blocks), jnp.int32),
@@ -262,14 +295,21 @@
             pltpu.SemaphoreType.DMA((4,)),
         ],
         params=WHOLE_PARAMS,
-    )(dest.reshape(1, blocks), counts.reshape(1, 1), cells, heights, weights)
-    arrived = lax.all_to_all(packed, ROW, split_axis=0, concat_axis=0, tiled=True)
+    )(side, dest.reshape(1, blocks), counts.reshape(1, 1), cells, heights, weights)
+    arrived = lax.all_to_all(
+        packed,
+        EVERY,
+        split_axis=0,
+        concat_axis=0,
+        tiled=True,
+        axis_index_groups=row_groups(lines, columns, rows),
+    )
 
     tall = tile_rows + 16
     slot = 2 * piece + 8
     parts = call(
         lambda *refs: strip_kernel(lines, columns, tile_rows, tile_cols, *refs),
-        jax.ShapeDtypeStruct((lines, columns, slot, tile_cols), f32),
+        jax.ShapeDtypeStruct((lines * columns, slot, tile_cols), f32),
         [VMEM_SPEC],
         (4 * rows * here * points * tile_rows * tile_cols, 4 * 4 * rows * here * points),
         [
@@ -278,20 +318,17 @@
             pltpu.VMEM((2, columns, tall, tile_cols), f32),
             pltpu.VMEM((2, tall, tile_cols), f32),
             pltpu.VMEM((2, tall, tile_cols), f32),
-            pltpu.VMEM((lines, columns, slot, tile_cols), f32),
-            pltpu.SemaphoreType.DMA((1,)),
         ],
-        out=HBM_SPEC,
     )(arrived)
     gathered = lax.all_to_all(
-        parts.reshape(lines * columns, slot, tile_cols),
-        ("line", "tile"),
+        parts,
+        EVERY,
         split_axis=0,
         concat_axis=0,
         tiled=True,
-    )
-
-    side = lax.axis_index("side").astype(jnp.int32).reshape(1, 1)
+        axis_index_groups=strip_groups(columns, rows),
+    )
+
     strips, cross = call(
         gather_kernel,
         [
@@ -303,7 +340,14 @@
     )(side, gathered)
     swap = [(i, i + 1) for i in range(1, rows - 1, 2)]
     cross = lax.ppermute(cross, ROW, swap + [(j, i) for i, j in swap])
-    strips = lax.all_to_all(strips, ("line", "side"), split_axis=0, concat_axis=0, tiled=True)
+    strips = lax.all_to_all(
+        strips,
+        EVERY,
+        split_axis=0,
+        concat_axis=0,
+        tiled=True,
+        axis_index_groups=end_groups(columns, rows),
+    )
 
     return call(
         finish_kernel,

time: 77.7 us -> 72.2 us (0.929)
  blocking collectives: 33.8 us -> 55 us
  starting transfers between devices: 18 us -> 4.73 us
  waiting for transfers between devices: 17.8 us -> 4.99 us
  Pallas kernels: 7 us -> 6.14 us
    all_to_all x1 -> x2, blocking collectives: 33.8 us -> 55 us  [the longest x1 34.5 us: per_device(): lax.all_to_all(packed, EVERY, split_axis=0, concat_axis=0, tiled=True, ax...]
    all_to_all x2 -> x1, starting transfers between devices: 17.3 us -> 4.08 us  [per_device(): lax.all_to_all(strips, EVERY, split_axis=0, concat_axis=0, tiled=True, ax...]
    all_to_all x2 -> x1, waiting for transfers between devices: 17.8 us -> 4.99 us  [per_device(): lax.all_to_all(strips, EVERY, split_axis=0, concat_axis=0, tiled=True, ax...]
    pallas_call x1, Pallas kernels: 3.68 us -> 2.82 us  [per_device(): call(lambda *refs: strip_kernel(lines, columns, tile_rows, tile_cols, *re...]
  transfers between devices with their start and end apart: 3 -> 2, of which waited for: 2 -> 1; matrix products, arithmetic and copies ran while one was open for 0% -> 0% of each run, Pallas kernels for 0% -> 0%
where the time goes in v5:
time: 72.2 us; the launch traced here: 71.5 us
  blocking collectives  55 us (76%)
  Pallas kernels  6.14 us (9%)
  waiting for transfers between devices  4.99 us (7%)
  starting transfers between devices  4.73 us (7%)
    all_to_all x1, blocking collectives, per_device(): lax.all_to_all(packed, EVERY, split_axis=0, concat_axis=0, tiled=True, ax...  34.5 us
    all_to_all x1, blocking collectives, per_device(): lax.all_to_all(parts, EVERY, split_axis=0, concat_axis=0, tiled=True, axi...  20.5 us
    all_to_all x1, waiting for transfers between devices, per_device(): lax.all_to_all(strips, EVERY, split_axis=0, concat_axis=0, tiled=True, ax...  4.99 us
    all_to_all x1, starting transfers between devices, per_device(): lax.all_to_all(strips, EVERY, split_axis=0, concat_axis=0, tiled=True, ax...  4.08 us
    pallas_call x1, Pallas kernels, per_device(): call(lambda *refs: strip_kernel(lines, columns, tile_rows, tile_cols, *re...  2.82 us
    pallas_call x1, Pallas kernels, per_device(): call(lambda *refs: pack_kernel(rows, columns, tile_cols, *refs), jax.Shap...  1.96 us
  transfers between devices with their start and end apart: 2, of which 1 were waited for; matrix products, arithmetic and copies ran while one was open for 0% of the time, Pallas kernels for 0%

profile of v5, /device:TPU:1, one launch (start us, length us, event | category | flops | bytes accessed | tf_op | source)
XLA Modules:
  0.0 71.5 jit_solution(2736951241546214121)
XLA Ops:
  0.7 2.0 %shard_map.64 = f32[16,48,128]{2,1,0:T(8,128)} custom-call(s32[1,1]{1,0:T(1,128)} %bitcast.refs_0_.side_ref, s32[1,128]{1,0:T(1,128)} %bitcast.4, s32[1,1]{1,0:T(1,128)} %bitcast.3.refs_2_, s32[128,128]{1,0:T(8,128)} %refs_3_.1, f32[128,128]{1,0:T(8,128)} %refs_4_.1, f32[128,128]{1,0:T(8,128)} %refs_5_.1), custom_call_target="tpu_custom_call" | custom-call | flops 33554432 | bytes 786432 | tf_op jit(solution)/shard_map/pallas_call | solution.py:285
  2.6 34.5 %all_to_all.15.refs_0_ = f32[16,48,128]{2,1,0:T(8,128)S(1)} all-to-all(f32[16,48,128]{2,1,0:T(8,128)} %shard_map.64), channel_id=1, replica_groups={{10,0,5,11,13,6,3,14,4,12,2,9,7,15,1,8},{26,16,21,27,29,22,19,30,20,28,..., dimensions={0} | all-to-all | bytes 786432 | tf_op jit(solution)/shard_map/all_to_all | solution.py:299
  37.1 2.8 %shard_map.65 = f32[32,40,128]{2,1,0:T(8,128)S(1)} custom-call(f32[16,48,128]{2,1,0:T(8,128)S(1)} %all_to_all.15.refs_0_), custom_call_target="tpu_custom_call" | custom-call | flops 1073741824 | bytes 524288 | tf_op jit(solution)/shard_map/pallas_call | solution.py:310
  39.9 20.5 %all_to_all.16.parts_ref = f32[32,40,128]{2,1,0:T(8,128)S(1)} all-to-all(f32[32,40,128]{2,1,0:T(8,128)S(1)} %shard_map.65), channel_id=1, replica_groups={{432,176,0,208,464,400,496,288,272,160,80,48,64,16,240,416,192,480,336,..., dimensions={0} | all-to-all | bytes 1310720 | tf_op jit(solution)/shard_map/all_to_all | solution.py:323
  60.4 0.7 shard_map.66
  61.2 0.0 copy-start
  61.2 4.1 %all-to-all-start.2 = ((f32[8,32,128]{2,1,0:T(8,128)}), f32[8,32,128]{2,1,0:T(8,128)S(1)}, u32[]{:S(2)}, u32[]{:S(2)}) async-start(f32[8,32,128]{2,1,0:T(8,128)} %get-tuple-element.7), calls=%async_computation.2 | async-start | bytes 262144 | tf_op jit(solution)/shard_map/all_to_all | solution.py:343
  65.2 0.6 collective-permute-start
  65.9 0.0 collective-permute-done.cross_ref
  65.9 5.0 %all-to-all-done.2.strips_ref = f32[8,32,128]{2,1,0:T(8,128)S(1)} async-done(((f32[8,32,128]{2,1,0:T(8,128)}), f32[8,32,128]{2,1,0:T(8,128)S(1)}, u32[]{:S(2)}, u32[]{:S(2)}) %all-to-all-start.2) | async-done | bytes 131104 | tf_op jit(solution)/shard_map/all_to_all | solution.py:343
  70.9 0.0 copy-done
  70.9 0.6 shard_map.67
Async XLA Ops:
  61.2 9.7 %copy-start = (f32[64,128]{1,0:T(8,128)S(1)}, f32[64,128]{1,0:T(8,128)}, u32[]{:S(2)}) copy-start(f32[64,128]{1,0:T(8,128)} %prefire_ref.1) | copy-start | bytes 98308
  61.2 9.7 %all-to-all-start.2 = ((f32[8,32,128]{2,1,0:T(8,128)}), f32[8,32,128]{2,1,0:T(8,128)S(1)}, u32[]{:S(2)}, u32[]{:S(2)}) async-start(f32[8,32,128]{2,1,0:T(8,128)} %get-tuple-element.7), calls=%async_computation.2 | async-start | bytes 262144 | tf_op jit(solution)/shard_map/all_to_all | solution.py:343
  65.2 0.7 collective-permute-start

commit v6 on v5

--- a/solution.py
+++ b/solution.py
@@ -15,7 +15,7 @@
 ROW = ("pair", "side")
 EVERY = ("line", "tile") + ROW
 ROW_ORDER = [10, 0, 5, 11, 13, 6, 3, 14, 4, 12, 2, 9, 7, 15, 1, 8]
-STRIP_ORDER = [27, 11, 0, 13, 29, 25, 31, 18, 17, 10, 5, 3, 4, 1, 15, 26, 12, 30, 21, 14, 2, 9, 28, 23, 8, 7, 16, 20, 24, 22, 19, 6]
+STRIP_ORDER = [27, 28, 29, 30, 31, 0, 1, 2, 3, 4, 5, 6, 7, 8, 9, 10, 11, 12, 13, 14, 15, 16, 17, 18, 19, 20, 21, 22, 23, 24, 25, 26]
 END_ORDER = [0, 1, 2, 3, 4, 5, 6, 7]
 
 

time: 72.2 us -> 71.6 us (level)
  blocking collectives: 55 us -> 54.1 us
    all_to_all x1, blocking collectives: 20.5 us -> 19.6 us  [per_device(): lax.all_to_all(parts, EVERY, split_axis=0, concat_axis=0, tiled=True, axi...]
where the time goes in v6:
time: 71.6 us; the launch traced here: 71.1 us
  blocking collectives  54.1 us (76%)
  Pallas kernels  6.14 us (9%)
  starting transfers between devices  5.17 us (7%)
  waiting for transfers between devices  4.98 us (7%)
    all_to_all x1, blocking collectives, per_device(): lax.all_to_all(packed, EVERY, split_axis=0, concat_axis=0, tiled=True, ax...  34.5 us
    all_to_all x1, blocking collectives, per_device(): lax.all_to_all(parts, EVERY, split_axis=0, concat_axis=0, tiled=True, axi...  19.6 us
    all_to_all x1, waiting for transfers between devices, per_device(): lax.all_to_all(strips, EVERY, split_axis=0, concat_axis=0, tiled=True, ax...  4.98 us
    all_to_all x1, starting transfers between devices, per_device(): lax.all_to_all(strips, EVERY, split_axis=0, concat_axis=0, tiled=True, ax...  4.52 us
    pallas_call x1, Pallas kernels, per_device(): call(lambda *refs: strip_kernel(lines, columns, tile_rows, tile_cols, *re...  2.82 us
    pallas_call x1, Pallas kernels, per_device(): call(lambda *refs: pack_kernel(rows, columns, tile_cols, *refs), jax.Shap...  1.96 us
  transfers between devices with their start and end apart: 2, of which 1 were waited for; matrix products, arithmetic and copies ran while one was open for 0% of the time, Pallas kernels for 0%

profile of v6, /device:TPU:1, one launch (start us, length us, event | category | flops | bytes accessed | tf_op | source)
XLA Modules:
  0.0 71.1 jit_solution(5543646635634015709)
XLA Ops:
  0.7 2.0 %shard_map.64 = f32[16,48,128]{2,1,0:T(8,128)} custom-call(s32[1,1]{1,0:T(1,128)} %bitcast.refs_0_.side_ref, s32[1,128]{1,0:T(1,128)} %bitcast.4, s32[1,1]{1,0:T(1,128)} %bitcast.3.refs_2_, s32[128,128]{1,0:T(8,128)} %refs_3_.1, f32[128,128]{1,0:T(8,128)} %refs_4_.1, f32[128,128]{1,0:T(8,128)} %refs_5_.1), custom_call_target="tpu_custom_call" | custom-call | flops 33554432 | bytes 786432 | tf_op jit(solution)/shard_map/pallas_call | solution.py:285
  2.6 34.5 %all_to_all.15.refs_0_ = f32[16,48,128]{2,1,0:T(8,128)S(1)} all-to-all(f32[16,48,128]{2,1,0:T(8,128)} %shard_map.64), channel_id=1, replica_groups={{10,0,5,11,13,6,3,14,4,12,2,9,7,15,1,8},{26,16,21,27,29,22,19,30,20,28,..., dimensions={0} | all-to-all | bytes 786432 | tf_op jit(solution)/shard_map/all_to_all | solution.py:299
  37.1 2.8 %shard_map.65 = f32[32,40,128]{2,1,0:T(8,128)S(1)} custom-call(f32[16,48,128]{2,1,0:T(8,128)S(1)} %all_to_all.15.refs_0_), custom_call_target="tpu_custom_call" | custom-call | flops 1073741824 | bytes 524288 | tf_op jit(solution)/shard_map/pallas_call | solution.py:310
  39.9 19.6 %all_to_all.16.parts_ref = f32[32,40,128]{2,1,0:T(8,128)S(1)} all-to-all(f32[32,40,128]{2,1,0:T(8,128)S(1)} %shard_map.65), channel_id=1, replica_groups={{432,448,464,480,496,0,16,32,48,64,80,96,112,128,144,160,176,192,208,22..., dimensions={0} | all-to-all | bytes 1310720 | tf_op jit(solution)/shard_map/all_to_all | solution.py:323
  59.6 0.7 %shard_map.66 = (f32[8,32,128]{2,1,0:T(8,128)}, f32[4,128]{1,0:T(4,128)S(1)}) custom-call(s32[1,1]{1,0:T(1,128)} %bitcast.refs_0_.side_ref, f32[32,40,128]{2,1,0:T(8,128)S(1)} %all_to_all.16.parts_ref), custom_call_target="tpu_custom_call" | custom-call | flops 163840 | bytes 655360 | tf_op jit(solution)/shard_map/pallas_call | solution.py:332
  60.3 0.0 copy-start
  60.3 4.5 %all-to-all-start.2 = ((f32[8,32,128]{2,1,0:T(8,128)}), f32[8,32,128]{2,1,0:T(8,128)S(1)}, u32[]{:S(2)}, u32[]{:S(2)}) async-start(f32[8,32,128]{2,1,0:T(8,128)} %get-tuple-element.7), calls=%async_computation.2 | async-start | bytes 262144 | tf_op jit(solution)/shard_map/all_to_all | solution.py:343
  64.8 0.6 collective-permute-start
  65.5 0.0 collective-permute-done.cross_ref
  65.5 5.0 %all-to-all-done.2.strips_ref = f32[8,32,128]{2,1,0:T(8,128)S(1)} async-done(((f32[8,32,128]{2,1,0:T(8,128)}), f32[8,32,128]{2,1,0:T(8,128)S(1)}, u32[]{:S(2)}, u32[]{:S(2)}) %all-to-all-start.2) | async-done | bytes 131104 | tf_op jit(solution)/shard_map/all_to_all | solution.py:343
  70.4 0.0 copy-done
  70.5 0.6 shard_map.67
Async XLA Ops:
  60.3 10.2 %copy-start = (f32[64,128]{1,0:T(8,128)S(1)}, f32[64,128]{1,0:T(8,128)}, u32[]{:S(2)}) copy-start(f32[64,128]{1,0:T(8,128)} %prefire_ref.1) | copy-start | bytes 98308
  60.3 10.2 %all-to-all-start.2 = ((f32[8,32,128]{2,1,0:T(8,128)}), f32[8,32,128]{2,1,0:T(8,128)S(1)}, u32[]{:S(2)}, u32[]{:S(2)}) async-start(f32[8,32,128]{2,1,0:T(8,128)} %get-tuple-element.7), calls=%async_computation.2 | async-start | bytes 262144 | tf_op jit(solution)/shard_map/all_to_all | solution.py:343
  64.8 0.7 collective-permute-start

commit v7 on v6

--- a/solution.py
+++ b/solution.py
@@ -116,7 +116,6 @@
     sources, held, points = in_ref.shape
     here = held // 3
     piece = tile_rows // lines
-    tall = tile_rows + 16
     first, end = 8, 8 + tile_rows
     cells = in_ref[:, 2 * here :, :].astype(jnp.int32)
     row_ref[...] = (cells // tile_cols).astype(jnp.float32)
@@ -128,9 +127,12 @@
     zero = jnp.zeros((tile_rows, points), jnp.bfloat16)
     one_col = jnp.ones((tile_cols, points), jnp.bfloat16)
     zero_col = jnp.zeros((tile_cols, points), jnp.bfloat16)
-    lane = lax.broadcasted_iota(jnp.int32, (tall, tile_cols), 1)
-    blank = jnp.zeros((tall, tile_cols), jnp.float32)
-    margin = jnp.zeros((8, tile_cols), jnp.float32)
+    lane = lax.broadcasted_iota(jnp.int32, (tile_rows, tile_cols), 1)
+    blank = jnp.zeros((tile_rows, tile_cols), jnp.float32)
+    margin = jnp.zeros((2, 8, tile_cols), jnp.float32)
+    for ref in (near_ref, far_ref):
+        ref[:, 0:first, :] = margin
+        ref[:, end:, :] = margin
 
     def spread(ref, source, at, count):
         line = ref[source, pl.ds(at, 1), :]
@@ -159,11 +161,7 @@
                 preferred_element_type=jnp.float32,
             )
         for value in range(2):
-            held_ref[value, column, 0:first, :] = margin
-            held_ref[value, column, first:end, :] = total[
-                value * tile_rows : (value + 1) * tile_rows, :
-            ]
-            held_ref[value, column, end:, :] = margin
+            held_ref[value, column] = total[value * tile_rows : (value + 1) * tile_rows, :]
 
     def turned(value, column):
         if column < 0 or column >= columns:
@@ -180,8 +178,8 @@
             lane >= tile_cols - 2, after[3], here[3]
         )
         same = 2.0 * x + one + 0.25 * two
-        near_ref[value] = x + 0.5 * one + 0.2 * two
-        far_ref[value] = 0.25 * x + 0.2 * one + 0.125 * two
+        near_ref[value, first:end, :] = x + 0.5 * one + 0.2 * two
+        far_ref[value, first:end, :] = 0.25 * x + 0.2 * one + 0.125 * two
 
         def near(at, count):
             return near_ref[value, at : at + count, :]
@@ -190,7 +188,7 @@
             return far_ref[value, at : at + count, :]
 
         inner = (
-            same[first:end, :]
+            same
             + near(first - 1, tile_rows)
             + near(first + 1, tile_rows)
             + far(first - 2, tile_rows)
@@ -315,7 +313,7 @@
         [
             pltpu.VMEM((rows, here, points), f32),
             pltpu.VMEM((rows, here, points), f32),
-            pltpu.VMEM((2, columns, tall, tile_cols), f32),
+            pltpu.VMEM((2, columns, tile_rows, tile_cols), f32),
             pltpu.VMEM((2, tall, tile_cols), f32),
             pltpu.VMEM((2, tall, tile_cols), f32),
         ],

time: 71.6 us -> 71.6 us (level)
  no operation moved by 1% of the time
where the time goes in v7:
time: 71.6 us; the launch traced here: 71 us
  blocking collectives  54.1 us (76%)
  Pallas kernels  6.08 us (8%)
  starting transfers between devices  5.17 us (7%)
  waiting for transfers between devices  4.98 us (7%)
    all_to_all x1, blocking collectives, per_device(): lax.all_to_all(packed, EVERY, split_axis=0, concat_axis=0, tiled=True, ax...  34.5 us
    all_to_all x1, blocking collectives, per_device(): lax.all_to_all(parts, EVERY, split_axis=0, concat_axis=0, tiled=True, axi...  19.6 us
    all_to_all x1, waiting for transfers between devices, per_device(): lax.all_to_all(strips, EVERY, split_axis=0, concat_axis=0, tiled=True, ax...  4.98 us
    all_to_all x1, starting transfers between devices, per_device(): lax.all_to_all(strips, EVERY, split_axis=0, concat_axis=0, tiled=True, ax...  4.52 us
    pallas_call x1, Pallas kernels, per_device(): call(lambda *refs: strip_kernel(lines, columns, tile_rows, tile_cols, *re...  2.77 us
    pallas_call x1, Pallas kernels, per_device(): call(lambda *refs: pack_kernel(rows, columns, tile_cols, *refs), jax.Shap...  1.96 us
  transfers between devices with their start and end apart: 2, of which 1 were waited for; matrix products, arithmetic and copies ran while one was open for 0% of the time, Pallas kernels for 0%

profile of v7, /device:TPU:1, one launch (start us, length us, event | category | flops | bytes accessed | tf_op | source)
XLA Modules:
  0.0 71.0 jit_solution(7458446946609928024)
XLA Ops:
  0.7 2.0 %shard_map.64 = f32[16,48,128]{2,1,0:T(8,128)} custom-call(s32[1,1]{1,0:T(1,128)} %bitcast.refs_0_.side_ref, s32[1,128]{1,0:T(1,128)} %bitcast.4, s32[1,1]{1,0:T(1,128)} %bitcast.3.refs_2_, s32[128,128]{1,0:T(8,128)} %refs_3_.1, f32[128,128]{1,0:T(8,128)} %refs_4_.1, f32[128,128]{1,0:T(8,128)} %refs_5_.1), custom_call_target="tpu_custom_call" | custom-call | flops 33554432 | bytes 786432 | tf_op jit(solution)/shard_map/pallas_call | solution.py:283
  2.6 34.5 %all_to_all.15.refs_0_ = f32[16,48,128]{2,1,0:T(8,128)S(1)} all-to-all(f32[16,48,128]{2,1,0:T(8,128)} %shard_map.64), channel_id=1, replica_groups={{10,0,5,11,13,6,3,14,4,12,2,9,7,15,1,8},{26,16,21,27,29,22,19,30,20,28,..., dimensions={0} | all-to-all | bytes 786432 | tf_op jit(solution)/shard_map/all_to_all | solution.py:297
  37.1 2.8 %shard_map.65 = f32[32,40,128]{2,1,0:T(8,128)S(1)} custom-call(f32[16,48,128]{2,1,0:T(8,128)S(1)} %all_to_all.15.refs_0_), custom_call_target="tpu_custom_call" | custom-call | flops 1073741824 | bytes 524288 | tf_op jit(solution)/shard_map/pallas_call | solution.py:308
  39.9 19.6 %all_to_all.16.parts_ref = f32[32,40,128]{2,1,0:T(8,128)S(1)} all-to-all(f32[32,40,128]{2,1,0:T(8,128)S(1)} %shard_map.65), channel_id=1, replica_groups={{432,448,464,480,496,0,16,32,48,64,80,96,112,128,144,160,176,192,208,22..., dimensions={0} | all-to-all | bytes 1310720 | tf_op jit(solution)/shard_map/all_to_all | solution.py:321
  59.5 0.7 %shard_map.66 = (f32[8,32,128]{2,1,0:T(8,128)}, f32[4,128]{1,0:T(4,128)S(1)}) custom-call(s32[1,1]{1,0:T(1,128)} %bitcast.refs_0_.side_ref, f32[32,40,128]{2,1,0:T(8,128)S(1)} %all_to_all.16.parts_ref), custom_call_target="tpu_custom_call" | custom-call | flops 163840 | bytes 655360 | tf_op jit(solution)/shard_map/pallas_call | solution.py:330
  60.2 0.0 copy-start
  60.2 4.5 %all-to-all-start.2 = ((f32[8,32,128]{2,1,0:T(8,128)}), f32[8,32,128]{2,1,0:T(8,128)S(1)}, u32[]{:S(2)}, u32[]{:S(2)}) async-start(f32[8,32,128]{2,1,0:T(8,128)} %get-tuple-element.7), calls=%async_computation.2 | async-start | bytes 262144 | tf_op jit(solution)/shard_map/all_to_all | solution.py:341
  64.7 0.6 collective-permute-start
  65.4 0.0 collective-permute-done.cross_ref
  65.4 5.0 %all-to-all-done.2.strips_ref = f32[8,32,128]{2,1,0:T(8,128)S(1)} async-done(((f32[8,32,128]{2,1,0:T(8,128)}), f32[8,32,128]{2,1,0:T(8,128)S(1)}, u32[]{:S(2)}, u32[]{:S(2)}) %all-to-all-start.2) | async-done | bytes 131104 | tf_op jit(solution)/shard_map/all_to_all | solution.py:341
  70.4 0.0 copy-done
  70.4 0.6 shard_map.67
Async XLA Ops:
  60.2 10.2 %copy-start = (f32[64,128]{1,0:T(8,128)S(1)}, f32[64,128]{1,0:T(8,128)}, u32[]{:S(2)}) copy-start(f32[64,128]{1,0:T(8,128)} %prefire_ref.1) | copy-start | bytes 98308
  60.2 10.2 %all-to-all-start.2 = ((f32[8,32,128]{2,1,0:T(8,128)}), f32[8,32,128]{2,1,0:T(8,128)S(1)}, u32[]{:S(2)}, u32[]{:S(2)}) async-start(f32[8,32,128]{2,1,0:T(8,128)} %get-tuple-element.7), calls=%async_computation.2 | async-start | bytes 262144 | tf_op jit(solution)/shard_map/all_to_all | solution.py:341
  64.7 0.7 collective-permute-start

commit v8 on v7

--- a/solution.py
+++ b/solution.py
@@ -136,7 +136,8 @@
 
     def spread(ref, source, at, count):
         line = ref[source, pl.ds(at, 1), :]
-        return jnp.broadcast_to(line, (count, points)).astype(jnp.bfloat16)
+        piece_rows = jnp.broadcast_to(line, (16, points)).astype(jnp.bfloat16)
+        return jnp.concatenate([piece_rows] * (count // 16), axis=0)
 
     def add_up(column):
         total = jnp.zeros((2 * tile_rows, tile_cols), jnp.float32)

time: 71.6 us -> 71.6 us (level)
  no operation moved by 1% of the time
where the time goes in v8:
time: 71.6 us; the launch traced here: 71 us
  blocking collectives  54.1 us (76%)
  Pallas kernels  6.08 us (8%)
  starting transfers between devices  5.17 us (7%)
  waiting for transfers between devices  4.98 us (7%)
    all_to_all x1, blocking collectives, per_device(): lax.all_to_all(packed, EVERY, split_axis=0, concat_axis=0, tiled=True, ax...  34.5 us
    all_to_all x1, blocking collectives, per_device(): lax.all_to_all(parts, EVERY, split_axis=0, concat_axis=0, tiled=True, axi...  19.6 us
    all_to_all x1, waiting for transfers between devices, per_device(): lax.all_to_all(strips, EVERY, split_axis=0, concat_axis=0, tiled=True, ax...  4.98 us
    all_to_all x1, starting transfers between devices, per_device(): lax.all_to_all(strips, EVERY, split_axis=0, concat_axis=0, tiled=True, ax...  4.52 us
    pallas_call x1, Pallas kernels, per_device(): call(lambda *refs: strip_kernel(lines, columns, tile_rows, tile_cols, *re...  2.77 us
    pallas_call x1, Pallas kernels, per_device(): call(lambda *refs: pack_kernel(rows, columns, tile_cols, *refs), jax.Shap...  1.96 us
  transfers between devices with their start and end apart: 2, of which 1 were waited for; matrix products, arithmetic and copies ran while one was open for 0% of the time, Pallas kernels for 0%

profile of v8, /device:TPU:1, one launch (start us, length us, event | category | flops | bytes accessed | tf_op | source)
XLA Modules:
  0.0 71.0 jit_solution(7458446946609928024)
XLA Ops:
  0.7 2.0 %shard_map.64 = f32[16,48,128]{2,1,0:T(8,128)} custom-call(s32[1,1]{1,0:T(1,128)} %bitcast.refs_0_.side_ref, s32[1,128]{1,0:T(1,128)} %bitcast.4, s32[1,1]{1,0:T(1,128)} %bitcast.3.refs_2_, s32[128,128]{1,0:T(8,128)} %refs_3_.1, f32[128,128]{1,0:T(8,128)} %refs_4_.1, f32[128,128]{1,0:T(8,128)} %refs_5_.1), custom_call_target="tpu_custom_call" | custom-call | flops 33554432 | bytes 786432 | tf_op jit(solution)/shard_map/pallas_call | solution.py:284
  2.6 34.5 %all_to_all.15.refs_0_ = f32[16,48,128]{2,1,0:T(8,128)S(1)} all-to-all(f32[16,48,128]{2,1,0:T(8,128)} %shard_map.64), channel_id=1, replica_groups={{10,0,5,11,13,6,3,14,4,12,2,9,7,15,1,8},{26,16,21,27,29,22,19,30,20,28,..., dimensions={0} | all-to-all | bytes 786432 | tf_op jit(solution)/shard_map/all_to_all | solution.py:298
  37.1 2.8 %shard_map.65 = f32[32,40,128]{2,1,0:T(8,128)S(1)} custom-call(f32[16,48,128]{2,1,0:T(8,128)S(1)} %all_to_all.15.refs_0_), custom_call_target="tpu_custom_call" | custom-call | flops 1073741824 | bytes 524288 | tf_op jit(solution)/shard_map/pallas_call | solution.py:309
  39.9 19.6 %all_to_all.16.parts_ref = f32[32,40,128]{2,1,0:T(8,128)S(1)} all-to-all(f32[32,40,128]{2,1,0:T(8,128)S(1)} %shard_map.65), channel_id=1, replica_groups={{432,448,464,480,496,0,16,32,48,64,80,96,112,128,144,160,176,192,208,22..., dimensions={0} | all-to-all | bytes 1310720 | tf_op jit(solution)/shard_map/all_to_all | solution.py:322
  59.5 0.7 %shard_map.66 = (f32[8,32,128]{2,1,0:T(8,128)}, f32[4,128]{1,0:T(4,128)S(1)}) custom-call(s32[1,1]{1,0:T(1,128)} %bitcast.refs_0_.side_ref, f32[32,40,128]{2,1,0:T(8,128)S(1)} %all_to_all.16.parts_ref), custom_call_target="tpu_custom_call" | custom-call | flops 163840 | bytes 655360 | tf_op jit(solution)/shard_map/pallas_call | solution.py:331
  60.2 0.0 copy-start
  60.2 4.5 %all-to-all-start.2 = ((f32[8,32,128]{2,1,0:T(8,128)}), f32[8,32,128]{2,1,0:T(8,128)S(1)}, u32[]{:S(2)}, u32[]{:S(2)}) async-start(f32[8,32,128]{2,1,0:T(8,128)} %get-tuple-element.7), calls=%async_computation.2 | async-start | bytes 262144 | tf_op jit(solution)/shard_map/all_to_all | solution.py:342
  64.7 0.6 collective-permute-start
  65.4 0.0 collective-permute-done.cross_ref
  65.4 5.0 %all-to-all-done.2.strips_ref = f32[8,32,128]{2,1,0:T(8,128)S(1)} async-done(((f32[8,32,128]{2,1,0:T(8,128)}), f32[8,32,128]{2,1,0:T(8,128)S(1)}, u32[]{:S(2)}, u32[]{:S(2)}) %all-to-all-start.2) | async-done | bytes 131104 | tf_op jit(solution)/shard_map/all_to_all | solution.py:342
  70.4 0.0 copy-done
  70.4 0.6 shard_map.67
Async XLA Ops:
  60.2 10.2 %copy-start = (f32[64,128]{1,0:T(8,128)S(1)}, f32[64,128]{1,0:T(8,128)}, u32[]{:S(2)}) copy-start(f32[64,128]{1,0:T(8,128)} %prefire_ref.1) | copy-start | bytes 98308
  60.2 10.2 %all-to-all-start.2 = ((f32[8,32,128]{2,1,0:T(8,128)}), f32[8,32,128]{2,1,0:T(8,128)S(1)}, u32[]{:S(2)}, u32[]{:S(2)}) async-start(f32[8,32,128]{2,1,0:T(8,128)} %get-tuple-element.7), calls=%async_computation.2 | async-start | bytes 262144 | tf_op jit(solution)/shard_map/all_to_all | solution.py:342
  64.7 0.7 collective-permute-start

commit v9 on v7

--- a/solution.py
+++ b/solution.py
@@ -99,8 +99,8 @@
         [
             (weights * heights_ref[...]).astype(jnp.bfloat16),
             weights.astype(jnp.bfloat16),
-            (cells // tile_cols).astype(jnp.float32).astype(jnp.bfloat16),
-            (cells % tile_cols).astype(jnp.float32).astype(jnp.bfloat16),
+            (cells >> (tile_cols.bit_length() - 1)).astype(jnp.float32).astype(jnp.bfloat16),
+            (cells & (tile_cols - 1)).astype(jnp.float32).astype(jnp.bfloat16),
         ],
         axis=1,
     )
@@ -118,8 +118,8 @@
     piece = tile_rows // lines
     first, end = 8, 8 + tile_rows
     cells = in_ref[:, 2 * here :, :].astype(jnp.int32)
-    row_ref[...] = (cells // tile_cols).astype(jnp.float32)
-    col_ref[...] = (cells % tile_cols).astype(jnp.float32)
+    row_ref[...] = (cells >> (tile_cols.bit_length() - 1)).astype(jnp.float32)
+    col_ref[...] = (cells & (tile_cols - 1)).astype(jnp.float32)
     row_ids = lax.broadcasted_iota(jnp.int32, (tile_rows, points), 0)
     row_ids = row_ids.astype(jnp.float32).astype(jnp.bfloat16)
     col_ids = lax.broadcasted_iota(jnp.int32, (tile_cols, points), 0)

time: 71.6 us -> 71.5 us (level)
  no operation moved by 1% of the time
where the time goes in v9:
time: 71.5 us; the launch traced here: 71 us
  blocking collectives  54.1 us (76%)
  Pallas kernels  6.01 us (8%)
  starting transfers between devices  5.15 us (7%)
  waiting for transfers between devices  4.98 us (7%)
    all_to_all x1, blocking collectives, per_device(): lax.all_to_all(packed, EVERY, split_axis=0, concat_axis=0, tiled=True, ax...  34.5 us
    all_to_all x1, blocking collectives, per_device(): lax.all_to_all(parts, EVERY, split_axis=0, concat_axis=0, tiled=True, axi...  19.6 us
    all_to_all x1, waiting for transfers between devices, per_device(): lax.all_to_all(strips, EVERY, split_axis=0, concat_axis=0, tiled=True, ax...  4.98 us
    all_to_all x1, starting transfers between devices, per_device(): lax.all_to_all(strips, EVERY, split_axis=0, concat_axis=0, tiled=True, ax...  4.5 us
    pallas_call x1, Pallas kernels, per_device(): call(lambda *refs: strip_kernel(lines, columns, tile_rows, tile_cols, *re...  2.73 us
    pallas_call x1, Pallas kernels, per_device(): call(lambda *refs: pack_kernel(rows, columns, tile_cols, *refs), jax.Shap...  1.92 us
  transfers between devices with their start and end apart: 2, of which 1 were waited for; matrix products, arithmetic and copies ran while one was open for 0% of the time, Pallas kernels for 0%

profile of v9, /device:TPU:1, one launch (start us, length us, event | category | flops | bytes accessed | tf_op | source)
XLA Modules:
  0.0 71.0 jit_solution(602915506097970447)
XLA Ops:
  0.7 1.9 %shard_map.64 = f32[16,48,128]{2,1,0:T(8,128)} custom-call(s32[1,1]{1,0:T(1,128)} %bitcast.refs_0_.side_ref, s32[1,128]{1,0:T(1,128)} %bitcast.4, s32[1,1]{1,0:T(1,128)} %bitcast.3.refs_2_, s32[128,128]{1,0:T(8,128)} %refs_3_.1, f32[128,128]{1,0:T(8,128)} %refs_4_.1, f32[128,128]{1,0:T(8,128)} %refs_5_.1), custom_call_target="tpu_custom_call" | custom-call | flops 33554432 | bytes 786432 | tf_op jit(solution)/shard_map/pallas_call | solution.py:283
  2.6 34.5 %all_to_all.15.refs_0_ = f32[16,48,128]{2,1,0:T(8,128)S(1)} all-to-all(f32[16,48,128]{2,1,0:T(8,128)} %shard_map.64), channel_id=1, replica_groups={{10,0,5,11,13,6,3,14,4,12,2,9,7,15,1,8},{26,16,21,27,29,22,19,30,20,28,..., dimensions={0} | all-to-all | bytes 786432 | tf_op jit(solution)/shard_map/all_to_all | solution.py:297
  37.1 2.7 %shard_map.65 = f32[32,40,128]{2,1,0:T(8,128)S(1)} custom-call(f32[16,48,128]{2,1,0:T(8,128)S(1)} %all_to_all.15.refs_0_), custom_call_target="tpu_custom_call" | custom-call | flops 1073741824 | bytes 524288 | tf_op jit(solution)/shard_map/pallas_call | solution.py:308
  39.8 19.6 %all_to_all.16.parts_ref = f32[32,40,128]{2,1,0:T(8,128)S(1)} all-to-all(f32[32,40,128]{2,1,0:T(8,128)S(1)} %shard_map.65), channel_id=1, replica_groups={{432,448,464,480,496,0,16,32,48,64,80,96,112,128,144,160,176,192,208,22..., dimensions={0} | all-to-all | bytes 1310720 | tf_op jit(solution)/shard_map/all_to_all | solution.py:321
  59.5 0.7 %shard_map.66 = (f32[8,32,128]{2,1,0:T(8,128)}, f32[4,128]{1,0:T(4,128)S(1)}) custom-call(s32[1,1]{1,0:T(1,128)} %bitcast.refs_0_.side_ref, f32[32,40,128]{2,1,0:T(8,128)S(1)} %all_to_all.16.parts_ref), custom_call_target="tpu_custom_call" | custom-call | flops 163840 | bytes 655360 | tf_op jit(solution)/shard_map/pallas_call | solution.py:330
  60.2 0.0 copy-start
  60.2 4.5 %all-to-all-start.2 = ((f32[8,32,128]{2,1,0:T(8,128)}), f32[8,32,128]{2,1,0:T(8,128)S(1)}, u32[]{:S(2)}, u32[]{:S(2)}) async-start(f32[8,32,128]{2,1,0:T(8,128)} %get-tuple-element.7), calls=%async_computation.2 | async-start | bytes 262144 | tf_op jit(solution)/shard_map/all_to_all | solution.py:341
  64.7 0.6 collective-permute-start
  65.3 0.0 collective-permute-done.cross_ref
  65.3 5.0 %all-to-all-done.2.strips_ref = f32[8,32,128]{2,1,0:T(8,128)S(1)} async-done(((f32[8,32,128]{2,1,0:T(8,128)}), f32[8,32,128]{2,1,0:T(8,128)S(1)}, u32[]{:S(2)}, u32[]{:S(2)}) %all-to-all-start.2) | async-done | bytes 131104 | tf_op jit(solution)/shard_map/all_to_all | solution.py:341
  70.3 0.0 copy-done
  70.3 0.6 shard_map.67
Async XLA Ops:
  60.2 10.2 %copy-start = (f32[64,128]{1,0:T(8,128)S(1)}, f32[64,128]{1,0:T(8,128)}, u32[]{:S(2)}) copy-start(f32[64,128]{1,0:T(8,128)} %prefire_ref.1) | copy-start | bytes 98308
  60.2 10.1 %all-to-all-start.2 = ((f32[8,32,128]{2,1,0:T(8,128)}), f32[8,32,128]{2,1,0:T(8,128)S(1)}, u32[]{:S(2)}, u32[]{:S(2)}) async-start(f32[8,32,128]{2,1,0:T(8,128)} %get-tuple-element.7), calls=%async_computation.2 | async-start | bytes 262144 | tf_op jit(solution)/shard_map/all_to_all | solution.py:341
  64.7 0.7 collective-permute-start
